TPU v7x, 256 devices: a whole 4x4x8 slice. The times are simulated.
256 devices in a mesh: row: 32 (over x, y, core), col: 8 (over z).
Axes of the slice: x: 4, y: 4, z: 8, core: 2. Of those that a mesh axis runs over, the one named last changes fastest.
Arguments:
- embeddings: bfloat16 [32768, 2048], P(('row', 'col')), may hold values from -6 to 6
- inverse_scales: float32 [2048], replicated, may hold values from 0.0039774757 to 0.059662133
- matches: int32 [32768, 2], replicated, may hold values from 0 to 32767
Outputs:
- trailing: float32 [32768, 4096], P('row', 'col')
- factor: float32 [32768, 1024], P(('row', 'col'))
Inputs may be any that keep to these rules, and one draw needn't show every extreme that they name: `matches`: candidate indices of the winner and the loser of each match.
All inputs are finite; a program needn't handle non-finite values.
Results may differ from a plain program's by a relative error of at most 0.0065.
Values may be sent and summed in bfloat16 or wider, within the bound.
A program may use at most 128 MiB of HBM per device.

v0:
```python
import math

import jax
import jax.numpy as jnp
from jax import lax
from jax.sharding import PartitionSpec as P

PANEL = 1024
STOPS = 4


def passed_along(block, axis, distance):
    devices = range(lax.axis_size(axis))
    route = [((i - distance) % len(devices), i) for i in devices]
    return lax.ppermute(block, axis, route)


def squares_of(scaled):
    values = scaled.astype(jnp.float32)
    return jnp.sum(values * values, axis=1)


def kernel_block(left, left_sq, right, right_sq):
    inner = jnp.dot(left, right.T, preferred_element_type=jnp.float32)
    return jnp.exp(-0.5 * (left_sq[:, None] + right_sq[None, :] - 2.0 * inner))


def match_counts(identity, matches):
    total = matches.shape[0]
    group_rows = math.gcd(total, 1024)
    grouped = matches.reshape(total // group_rows, group_rows, 2)

    def accumulate(carry, group):
        hits = (group[:, 0:1] == identity[None, :]).astype(jnp.float32)
        hits = hits + (group[:, 1:2] == identity[None, :]).astype(jnp.float32)
        return (carry + jnp.sum(hits, axis=0), None)

    counts, unused = lax.scan(accumulate, jnp.zeros(identity.shape, jnp.float32), grouped)
    return 0.1 + 0.5 * counts


def with_extras(block, row_ids, column_ids, row_extra):
    return block + jnp.where(row_ids[:, None] == column_ids[None, :], row_extra[:, None], 0.0)


def solve_rows(lower, rows):
    return lax.linalg.triangular_solve(lower, rows, left_side=False, lower=True, transpose_a=True)


def body(embeddings, inverse_scales, matches):
    row_count = lax.axis_size("row")
    col_count = lax.axis_size("col")
    row_index = lax.axis_index("row")
    col_index = lax.axis_index("col")
    slice_rows = embeddings.shape[0]
    block_rows = slice_rows * col_count
    panel_share = PANEL // row_count
    scaled = (embeddings.astype(jnp.float32) * inverse_scales[None, :]).astype(jnp.bfloat16)
    own_sq = squares_of(scaled)
    own_ids = (
        row_index * block_rows + col_index * slice_rows + jnp.arange(slice_rows, dtype=jnp.int32)
    )
    own_extra = match_counts(own_ids, matches)
    block_scaled = lax.all_gather(scaled, "col", axis=0, tiled=True)
    block_sq = squares_of(block_scaled)
    lead_scaled = block_scaled[:panel_share]
    panel_scaled = lax.all_gather(lead_scaled, "row", axis=0, tiled=True)
    panel_sq = squares_of(panel_scaled)
    panel_ids = (
        jnp.arange(row_count, dtype=jnp.int32)[:, None] * block_rows
        + jnp.arange(panel_share, dtype=jnp.int32)[None, :]
    ).reshape(-1)
    lead_ids = row_index * block_rows + jnp.arange(panel_share, dtype=jnp.int32)
    leading = with_extras(
        kernel_block(lead_scaled, block_sq[:panel_share], panel_scaled, panel_sq),
        lead_ids,
        panel_ids,
        match_counts(lead_ids, matches),
    )
    diagonal = lax.all_gather(leading, "row", axis=0, tiled=True)
    lower = jnp.linalg.cholesky(diagonal)
    own_rows = with_extras(
        kernel_block(scaled, own_sq, panel_scaled, panel_sq), own_ids, panel_ids, own_extra
    )
    own_factor = solve_rows(lower, own_rows)
    block_factor = lax.all_gather(own_factor, "col", axis=0, tiled=True)

    def stop_tile(visit_scaled, visit_factor):
        tile = kernel_block(block_scaled, block_sq, visit_scaled, squares_of(visit_scaled))
        return tile - jnp.dot(block_factor, visit_factor.T, precision=lax.Precision.HIGHEST)

    local_cols = col_index * slice_rows + jnp.arange(slice_rows, dtype=jnp.int32)
    first = stop_tile(scaled, own_factor)
    first = first + jnp.where(
        jnp.arange(block_rows, dtype=jnp.int32)[:, None] == local_cols[None, :],
        own_extra[None, :],
        0.0,
    )
    pieces = [first]
    visitor = (scaled, own_factor)
    for stop in range(1, STOPS):
        visitor = (
            passed_along(visitor[0].astype(jnp.float32), "row", 1).astype(jnp.bfloat16),
            passed_along(visitor[1], "row", 1),
        )
        pieces.append(stop_tile(visitor[0], visitor[1]))
    trailing = jnp.concatenate(pieces, axis=1)
    return (trailing, own_factor)


def solution(mesh):
    return jax.shard_map(
        body,
        mesh=mesh,
        in_specs=(P(("row", "col"), None), P(), P()),
        out_specs=(P("row", "col"), P(("row", "col"), None)),
        check_vma=False,
    )
```

profile of v0, /device:TPU:1, one launch (start us, length us, event | category | flops | bytes accessed | tf_op | source)
XLA Modules:
  0.0 597.3 jit_solution(3728783315222918440)
XLA Ops:
  9.3 59.7 %all-gather.5.cloned.1.call-done = bf16[1024,2048]{1,0:T(8,128)(2,1)} async-done(((bf16[128,2048]{1,0:T(8,128)(2,1)}), bf16[1024,2048]{1,0:T(8,128)(2,1)}) %all-gather.5.cloned.1.call-update) | async-done | bytes 4194320 | tf_op jit(solution)/shard_map/all_gather | solution.py:64
  70.7 30.5 %while.25 = (s32[]{:T(128)}, f32[32]{0:T(128)S(1)}, s32[32,1024,2]{1,2,0:T(2,128)}, s32[]{:T(128)}, s32[]{:T(128)}, /*index=5*/s32[]{:T(128)}) while((s32[]{:T(128)}, f32[32]{0:T(128)S(1)}, s32[32,1024,2]{1,2,0:T(2,128)}, s32[]{:T(128)}, s32[]{:T(128)}, /*index=5*/s32[]{:T(128)}) %tuple.122), condition=%wide.region_8.9_spmd.clone, body=%wide.region_6.8_spmd.clone.sunk | while | flops 196675 | bytes 41823 | solution.py:38
  104.4 17.9 %all-gather.7.cloned.1.call-done = bf16[1024,2048]{1,0:T(8,128)(2,1)} async-done(((bf16[32,2048]{1,0:T(8,128)(2,1)}), bf16[1024,2048]{1,0:T(8,128)(2,1)}) %all-gather.7.cloned.1.call-update) | async-done | bytes 4194320 | tf_op jit(solution)/shard_map/all_gather | solution.py:67
  128.8 35.4 %while.24 = (s32[]{:T(128)}, f32[128]{0:T(128)S(1)}, s32[32,1024,2]{1,2,0:T(2,128)}, s32[]{:T(128)}, s32[]{:T(128)}, /*index=5*/s32[]{:T(128)}) while((s32[]{:T(128)}, f32[128]{0:T(128)S(1)}, s32[32,1024,2]{1,2,0:T(2,128)}, s32[]{:T(128)}, s32[]{:T(128)}, /*index=5*/s32[]{:T(128)}) %tuple.123), condition=%wide.region_5.6_spmd.clone, body=%wide.region_3.0_spmd.clone.sunk | while | flops 786691 | bytes 44127 | solution.py:38
  168.0 11.5 %all-gather.9.cloned.1.call-done = f32[1024,1024]{1,0:T(8,128)} async-done(((f32[32,1024]{1,0:T(8,128)}), f32[1024,1024]{1,0:T(8,128)}) %all-gather.9.cloned.1.call-update) | async-done | bytes 4194320 | tf_op jit(solution)/shard_map/all_gather | solution.py:80
  179.5 5.5 copy.12
  185.0 4.4 fusion.6
  191.4 11.7 %cholesky.223 = f32[128,128]{1,0:T(8,128)S(1)} custom-call(f32[128,128]{1,0:T(8,128)S(1)} %cholesky.580), custom_call_target="Cholesky" | custom-call | tf_op jit(solution)/shard_map/jit(cholesky)/cholesky | solution.py:81
  203.1 9.8 %custom-call.62 = f32[1,128,128]{1,2,0:T(8,128)S(1)} custom-call(f32[1,128,128]{2,1,0:T(8,128)S(1)} %get-tuple-element.176), custom_call_target="InvertDiagBlocksLowerTriangular" | custom-call | tf_op jit(solution)/shard_map/jit(cholesky)/cholesky | solution.py:81
  219.4 11.9 %cholesky.244 = f32[128,128]{1,0:T(8,128)S(1)} custom-call(f32[128,128]{1,0:T(8,128)S(1)} %cholesky.584), custom_call_target="Cholesky" | custom-call | tf_op jit(solution)/shard_map/jit(cholesky)/cholesky | solution.py:81
  231.9 9.8 %custom-call.63 = f32[1,128,128]{1,2,0:T(8,128)S(1)} custom-call(f32[1,128,128]{2,1,0:T(8,128)S(1)} %get-tuple-element.173), custom_call_target="InvertDiagBlocksLowerTriangular" | custom-call | tf_op jit(solution)/shard_map/jit(cholesky)/cholesky | solution.py:81
  245.1 11.7 %cholesky.468 = f32[128,128]{1,0:T(8,128)S(1)} custom-call(f32[128,128]{1,0:T(8,128)S(1)} %cholesky.589), custom_call_target="Cholesky" | custom-call | tf_op jit(solution)/shard_map/jit(cholesky)/cholesky | solution.py:81
  258.1 9.8 %custom-call.64 = f32[1,128,128]{1,2,0:T(8,128)S(1)} custom-call(f32[1,128,128]{2,1,0:T(8,128)S(1)} %get-tuple-element.170), custom_call_target="InvertDiagBlocksLowerTriangular" | custom-call | tf_op jit(solution)/shard_map/jit(cholesky)/cholesky | solution.py:81
  271.5 12.1 %cholesky.487 = f32[128,128]{1,0:T(8,128)S(1)} custom-call(f32[128,128]{1,0:T(8,128)S(1)} %cholesky.594), custom_call_target="Cholesky" | custom-call | tf_op jit(solution)/shard_map/jit(cholesky)/cholesky | solution.py:81
  284.9 9.8 %custom-call.65 = f32[1,128,128]{1,2,0:T(8,128)S(1)} custom-call(f32[1,128,128]{2,1,0:T(8,128)S(1)} %get-tuple-element.167), custom_call_target="InvertDiagBlocksLowerTriangular" | custom-call | tf_op jit(solution)/shard_map/jit(cholesky)/cholesky | solution.py:81
  298.2 11.7 %cholesky.506 = f32[128,128]{1,0:T(8,128)S(1)} custom-call(f32[128,128]{1,0:T(8,128)S(1)} %cholesky.599), custom_call_target="Cholesky" | custom-call | tf_op jit(solution)/shard_map/jit(cholesky)/cholesky | solution.py:81
  311.3 9.9 %custom-call.66 = f32[1,128,128]{1,2,0:T(8,128)S(1)} custom-call(f32[1,128,128]{2,1,0:T(8,128)S(1)} %get-tuple-element.164), custom_call_target="InvertDiagBlocksLowerTriangular" | custom-call | tf_op jit(solution)/shard_map/jit(cholesky)/cholesky | solution.py:81
  324.5 11.7 %cholesky.526 = f32[128,128]{1,0:T(8,128)S(1)} custom-call(f32[128,128]{1,0:T(8,128)S(1)} %cholesky.604), custom_call_target="Cholesky" | custom-call | tf_op jit(solution)/shard_map/jit(cholesky)/cholesky | solution.py:81
  337.6 9.8 %custom-call.67 = f32[1,128,128]{1,2,0:T(8,128)S(1)} custom-call(f32[1,128,128]{2,1,0:T(8,128)S(1)} %get-tuple-element.161), custom_call_target="InvertDiagBlocksLowerTriangular" | custom-call | tf_op jit(solution)/shard_map/jit(cholesky)/cholesky | solution.py:81
  350.4 11.9 %cholesky.546 = f32[128,128]{1,0:T(8,128)S(1)} custom-call(f32[128,128]{1,0:T(8,128)S(1)} %cholesky.609), custom_call_target="Cholesky" | custom-call | tf_op jit(solution)/shard_map/jit(cholesky)/cholesky | solution.py:81
  363.6 9.8 %custom-call.68 = f32[1,128,128]{1,2,0:T(8,128)S(1)} custom-call(f32[1,128,128]{2,1,0:T(8,128)S(1)} %get-tuple-element.158), custom_call_target="InvertDiagBlocksLowerTriangular" | custom-call | tf_op jit(solution)/shard_map/jit(cholesky)/cholesky | solution.py:81
  376.0 11.7 %cholesky.564 = f32[128,128]{1,0:T(8,128)S(1)} custom-call(f32[128,128]{1,0:T(8,128)S(1)} %convolution_subtract_fusion.15), custom_call_target="Cholesky" | custom-call | tf_op jit(solution)/shard_map/jit(cholesky)/cholesky | solution.py:81
  394.8 4.8 select_select_fusion
  399.7 23.2 %while.23 = (s32[]{:T(128)}, f32[1024,1024]{1,0:T(8,128)}, s32[8,2]{0,1:T(2,128)S(1)}, f32[8,128,128]{2,1,0:T(8,128)S(1)}, s32[]{:T(128)}) while((s32[]{:T(128)}, f32[1024,1024]{1,0:T(8,128)}, s32[8,2]{0,1:T(2,128)S(1)}, f32[8,128,128]{2,1,0:T(8,128)S(1)}, s32[]{:T(128)}) %tuple.108), condition=%wide.while_cond, body=%wide.while_body.sunk | while | flops 2 | bytes 131189 | solution.py:47
  422.9 79.0 %custom-call.69 = f32[8,128,128]{1,2,0:T(8,128)S(1)} custom-call(f32[8,128,128]{2,1,0:T(8,128)S(1)} %get-tuple-element.55), custom_call_target="InvertDiagBlocksLowerTriangular" | custom-call | tf_op jit(solution)/shard_map/triangular_solve | solution.py:47
  517.0 6.1 %collective-permute-done = bf16[128,2048]{1,0:T(8,128)(2,1)S(1)} collective-permute-done((bf16[128,2048]{1,0:T(8,128)(2,1)S(1)}, bf16[128,2048]{1,0:T(8,128)(2,1)S(1)}, u32[]{:S(2)}, u32[]{:S(2)}) %collective-permute-start) | collective-permute-done | bytes 524320 | tf_op jit(solution)/shard_map/ppermute | solution.py:15
  525.7 6.1 %collective-permute-done.2 = bf16[128,2048]{1,0:T(8,128)(2,1)S(1)} collective-permute-done((bf16[128,2048]{1,0:T(8,128)(2,1)S(1)}, bf16[128,2048]{1,0:T(8,128)(2,1)S(1)}, u32[]{:S(2)}, u32[]{:S(2)}) %collective-permute-start.2) | collective-permute-done | bytes 524320 | tf_op jit(solution)/shard_map/ppermute | solution.py:15
  534.6 6.9 %collective-permute-done.4 = bf16[128,2048]{1,0:T(8,128)(2,1)S(1)} collective-permute-done((bf16[128,2048]{1,0:T(8,128)(2,1)S(1)}, bf16[128,2048]{1,0:T(8,128)(2,1)S(1)}, u32[]{:S(2)}, u32[]{:S(2)}) %collective-permute-start.4) | collective-permute-done | bytes 524320 | tf_op jit(solution)/shard_map/ppermute | solution.py:15
  548.5 5.5 collective-permute-done.1
  559.0 7.0 %collective-permute-done.3 = f32[128,1024]{0,1:T(8,128)S(1)} collective-permute-done((f32[128,1024]{0,1:T(8,128)S(1)}, f32[128,1024]{0,1:T(8,128)S(1)}, u32[]{:S(2)}, u32[]{:S(2)}) %collective-permute-start.3) | collective-permute-done | bytes 524320 | tf_op jit(solution)/shard_map/ppermute | solution.py:15
  566.0 8.8 %all-gather.11.cloned.1.call-done = f32[1024,1024]{0,1:T(8,128)} async-done(((f32[128,1024]{0,1:T(8,128)}), f32[1024,1024]{0,1:T(8,128)}) %all-gather.11.cloned.1.call-update) | async-done | bytes 4194320 | tf_op jit(solution)/shard_map/all_gather | solution.py:86
  574.9 4.9 convolution_subtract_fusion.2
  (460 shorter events, 184.7 us)
Async XLA Ops:
  7.2 61.9 %all-gather.5.cloned.1.call-start = ((), (), s32[]{:S(2)}) async-start(), calls=%async_computation | async-start | bytes 4718592 | tf_op jit(solution)/shard_map/all_gather | solution.py:64
  9.2 113.1 %all-gather.7.cloned.1.call-start = ((), (), s32[]{:S(2)}) async-start(), calls=%async_computation.1 | async-start | bytes 4325376 | tf_op jit(solution)/shard_map/all_gather | solution.py:67
  70.6 108.9 %all-gather.9.cloned.1.call-start = ((), (), s32[]{:S(2)}) async-start(), calls=%async_computation.2 | async-start | bytes 4325376 | tf_op jit(solution)/shard_map/all_gather | solution.py:80
  122.4 3.4 copy-start.1
  122.4 41.9 %copy-start.6 = (bf16[128,2048]{1,0:T(8,128)(2,1)S(1)}, bf16[128,2048]{1,0:T(8,128)(2,1)}, u32[]{:S(2)}) copy-start(bf16[128,2048]{1,0:T(8,128)(2,1)} %get-tuple-element.123) | copy-start | bytes 1572868
  128.8 446.1 %all-gather.11.cloned.1.call-start = ((), (), s32[]{:S(2)}) async-start(), calls=%async_computation.3 | async-start | bytes 4718592 | tf_op jit(solution)/shard_map/all_gather | solution.py:86
  189.4 2.0 copy-start.2
  515.1 0.8 copy-start.3
  515.9 7.2 %collective-permute-start = (bf16[128,2048]{1,0:T(8,128)(2,1)S(1)}, bf16[128,2048]{1,0:T(8,128)(2,1)S(1)}, u32[]{:S(2)}, u32[]{:S(2)}) collective-permute-start(bf16[128,2048]{1,0:T(8,128)(2,1)S(1)} %copy-done.6), channel_id=1, source_target_pairs={{248,0},{0,8},{8,16},{16,24},{24,32},{32,40},{40,48},{48,56},{56,6... | collective-permute-start | bytes 1572872 | tf_op jit(solution)/shard_map/ppermute | solution.py:15
  523.2 8.6 %collective-permute-start.2 = (bf16[128,2048]{1,0:T(8,128)(2,1)S(1)}, bf16[128,2048]{1,0:T(8,128)(2,1)S(1)}, u32[]{:S(2)}, u32[]{:S(2)}) collective-permute-start(bf16[128,2048]{1,0:T(8,128)(2,1)S(1)} %collective-permute-done), channel_id=1, source_target_pairs={{248,0},{0,8},{8,16},{16,24},{24,32},{32,40},{40,48},{48,56},{56,6... | collective-permute-start | bytes 1572872 | tf_op jit(solution)/shard_map/ppermute | solution.py:15
  531.8 9.8 %collective-permute-start.4 = (bf16[128,2048]{1,0:T(8,128)(2,1)S(1)}, bf16[128,2048]{1,0:T(8,128)(2,1)S(1)}, u32[]{:S(2)}, u32[]{:S(2)}) collective-permute-start(bf16[128,2048]{1,0:T(8,128)(2,1)S(1)} %collective-permute-done.2), channel_id=1, source_target_pairs={{248,0},{0,8},{8,16},{16,24},{24,32},{32,40},{40,48},{48,56},{56,6... | collective-permute-start | bytes 1572872 | tf_op jit(solution)/shard_map/ppermute | solution.py:15
  534.4 12.5 %copy-start.5 = (bf16[1024,2048]{1,0:T(8,128)(2,1)S(1)}, bf16[1024,2048]{1,0:T(8,128)(2,1)}, u32[]{:S(2)}) copy-start(bf16[1024,2048]{1,0:T(8,128)(2,1)} %all-gather.5.cloned.1.call-done) | copy-start | bytes 12582916
  541.7 12.2 %collective-permute-start.1 = (f32[128,1024]{0,1:T(8,128)}, f32[128,1024]{0,1:T(8,128)S(1)}, u32[]{:S(2)}, u32[]{:S(2)}) collective-permute-start(f32[128,1024]{0,1:T(8,128)} %copy-done.3), channel_id=1, source_target_pairs={{248,0},{0,8},{8,16},{16,24},{24,32},{32,40},{40,48},{48,56},{56,6... | collective-permute-start | bytes 1572872 | tf_op jit(solution)/shard_map/ppermute | solution.py:15
  553.9 12.1 %collective-permute-start.3 = (f32[128,1024]{0,1:T(8,128)S(1)}, f32[128,1024]{0,1:T(8,128)S(1)}, u32[]{:S(2)}, u32[]{:S(2)}) collective-permute-start(f32[128,1024]{0,1:T(8,128)S(1)} %collective-permute-done.1), channel_id=1, source_target_pairs={{248,0},{0,8},{8,16},{16,24},{24,32},{32,40},{40,48},{48,56},{56,6... | collective-permute-start | bytes 1572872 | tf_op jit(solution)/shard_map/ppermute | solution.py:15
  556.5 1.6 copy-start.4
  566.0 19.0 %collective-permute-start.5 = (f32[128,1024]{0,1:T(8,128)S(1)}, f32[128,1024]{0,1:T(8,128)}, u32[]{:S(2)}, u32[]{:S(2)}) collective-permute-start(f32[128,1024]{0,1:T(8,128)S(1)} %collective-permute-done.3), channel_id=1, source_target_pairs={{248,0},{0,8},{8,16},{16,24},{24,32},{32,40},{40,48},{48,56},{56,6... | collective-permute-start | bytes 1572872 | tf_op jit(solution)/shard_map/ppermute | solution.py:15
  574.8 4.9 copy-start
  574.9 4.9 copy-start.7
Sparse Core Ops, SparseCore 0:
  10.4 58.6 all-gather.4
  72.1 50.1 all-gather.6
  128.9 50.5 all-gather.8
  516.1 58.7 all-gather.10
where the time goes:
time: 608 us; the launch traced here: 597 us
  other arithmetic  289 us (48%)
  waiting for transfers between devices  130 us (21%)
  local copies, waits for them, and re-layouts  84.2 us (14%)
  matrix products  65.9 us (11%)
  between operations  19.6 us (3%)
  starting transfers between devices  7.78 us (1%)
    another operation x30, other arithmetic, body(): lower = jnp.linalg.cholesky(diagonal)  173 us
    another operation x3, other arithmetic, solve_rows(): lax.linalg.triangular_solve(lower, rows, left_side=False, lower=True, tra...  83.8 us
    all_gather x1, waiting for transfers between devices, body(): block_scaled = lax.all_gather(scaled, 'col', axis=0, tiled=True)  59.7 us
    squeeze x64, local copies, waits for them, and re-layouts, match_counts(): lax.scan(accumulate, jnp.zeros(identity.shape, jnp.float32), grouped)  45 us
    ppermute x6, waiting for transfers between devices, passed_along(): return lax.ppermute(block, axis, route)  31.6 us
    another operation x14, matrix products, body(): lower = jnp.linalg.cholesky(diagonal)  23.1 us
    another operation x24, local copies, waits for them, and re-layouts  23 us
    all_gather x1, waiting for transfers between devices, body(): panel_scaled = lax.all_gather(lead_scaled, 'row', axis=0, tiled=True)  17.9 us
  transfers between devices with their start and end apart: 10, of which 9 were waited for; matrix products, arithmetic and copies ran while one was open for 15% of the time, Pallas kernels for 0%

commit v1 on v0

v1 whole, which is shorter than its diff:
```python
import functools

import jax
import jax.numpy as jnp
from jax import lax
from jax.experimental import pallas as pl
from jax.experimental.pallas import tpu as pltpu
from jax.sharding import PartitionSpec as P

PANEL = 1024
STOPS = 4
LEAF = 128
AHEAD = 4
F32 = jnp.float32
BF16 = jnp.bfloat16


def halves(x):
    high = x.astype(BF16)
    return high, (x - high.astype(F32)).astype(BF16)


def dot(a, b):
    return jnp.dot(a, b, preferred_element_type=F32)


def dot_nt(a, b):
    return lax.dot_general(a, b, (((1,), (1,)), ((), ())), preferred_element_type=F32)


def leaf_factor(tile, out_ref):
    n = LEAF
    groups = n // 8
    lane = lax.broadcasted_iota(jnp.int32, (8, 128), 1)
    rows = [tile[8 * i : 8 * i + 8, :] for i in range(groups)]

    def column(i, k):
        return jnp.broadcast_to(rows[i][:, k : k + 1], (8, 128))

    def one_row(x, r):
        return jnp.broadcast_to(x[r : r + 1, :], (8, 128))

    pending = [[column(i, k) for i in range(groups)] for k in range(AHEAD)]
    for k in range(n):
        g, r = divmod(k, 8)
        current = pending.pop(0)
        scale = lax.rsqrt(one_row(current[g], r))
        c = [current[i] * scale if i >= g else None for i in range(groups)]
        if k + AHEAD < n:
            pending.append([column(i, k + AHEAD) if i >= (k + AHEAD) // 8 else None for i in range(groups)])
        for j in range(len(pending)):
            gp, rp = divmod(k + 1 + j, 8)
            s = one_row(c[gp], rp)
            pending[j] = [pending[j][i] - c[i] * s if i >= gp else None for i in range(groups)]
        u = jnp.where(lane == k, scale, one_row(rows[g], r) * scale)
        out_ref[k : k + 1, :] = u[0:1, :]
        for i in range(g, groups):
            rows[i] = jnp.where(lane == k, 0.0, rows[i]) - c[i] * u


def count_kernel(base, matches_ref, out_ref, hits):
    first = base()

    def step(i, unused):
        ids = [first + 4 * i + q for q in range(4)]
        totals = [jnp.zeros((8, 128), F32) for q in range(4)]
        for block in range(matches_ref.shape[0] // 8):
            values = matches_ref[8 * block : 8 * block + 8, :]
            for q in range(4):
                totals[q] = totals[q] + jnp.where(values == ids[q], 1.0, 0.0)
        for q in range(4):
            hits[pl.ds(4 * i + q, 1), :] = jnp.sum(totals[q], axis=0, keepdims=True)
        return unused

    lax.fori_loop(0, 32, step, 0)
    out_ref[...] = jnp.broadcast_to(jnp.sum(hits[...].T, axis=0, keepdims=True), (8, 128))


def match_counts(matches):
    def base():
        return (lax.axis_index("row") * lax.axis_size("col") + lax.axis_index("col")) * LEAF

    return pl.pallas_call(
        functools.partial(count_kernel, base),
        out_shape=jax.ShapeDtypeStruct((8, 128), F32),
        in_specs=[pl.BlockSpec(memory_space=pltpu.VMEM)],
        out_specs=pl.BlockSpec(memory_space=pltpu.VMEM),
        scratch_shapes=[pltpu.VMEM((128, 128), F32)],
        name="match_counts",
    )(matches)


def squares_column(x_ref, start, count, chunk=128):
    parts = []
    for i in range(count // chunk):
        v = x_ref[start + i * chunk : start + (i + 1) * chunk, :].astype(F32)
        parts.append(jnp.sum(v * v, axis=1, keepdims=True))
    return parts


def to_lanes(column):
    return jnp.broadcast_to(column, (128, 128)).T[0:1, :]


def chain_kernel(panel_ref, extra_ref, xh_ref, xl_ref, sq_ref, a, leaf, low, sq_col):
    count = PANEL // LEAF
    for i in range(count):
        v = panel_ref[i * LEAF : (i + 1) * LEAF, :].astype(F32)
        s = jnp.sum(v * v, axis=1, keepdims=True)
        sq_col[i * LEAF : (i + 1) * LEAF, :] = jnp.broadcast_to(s, (LEAF, 128))
        sq_ref[0:1, i * LEAF : (i + 1) * LEAF] = to_lanes(s)
    row = lax.broadcasted_iota(jnp.int32, (PANEL, 256), 0)
    lane = lax.broadcasted_iota(jnp.int32, (PANEL, 256), 1)

    def build(n, unused):
        cols = pl.ds(pl.multiple_of(n * 256, 256), 256)
        g = dot_nt(panel_ref[...], panel_ref[cols, :])
        s = sq_col[...]
        k = jnp.exp(-0.5 * (jnp.concatenate([s, s], axis=1) + sq_ref[0:1, cols] - 2.0 * g))
        a[:, cols] = k + jnp.where(row == lane + n * 256, extra_ref[0:1, cols], 0.0)
        return unused

    lax.fori_loop(0, PANEL // 256, build, 0)
    r128 = lax.broadcasted_iota(jnp.int32, (LEAF, LEAF), 0)
    c128 = lax.broadcasted_iota(jnp.int32, (LEAF, LEAF), 1)

    def step(k, unused):
        own = pl.ds(pl.multiple_of(k * LEAF, LEAF), LEAF)
        leaf_factor(a[own, own], leaf)
        w = jnp.where(r128 >= c128, leaf[...], 0.0)
        wt = w.T
        wh, wl = halves(w)
        th, tl = halves(wt)
        w3 = jnp.concatenate([wh, wh, wl], axis=1)
        t3 = jnp.concatenate([th, tl, th], axis=0)
        ch, cl = halves(a[:, own])
        lcol = dot(jnp.concatenate([ch, ch, cl], axis=1), t3)
        a[:, own] = lcol
        a[own, own] = wt
        lh, ll = halves(lcol)
        low[:, 0:LEAF] = lh
        low[:, LEAF : 2 * LEAF] = lh
        low[:, 2 * LEAF :] = ll
        low[own, 0:LEAF] = th
        low[own, LEAF : 2 * LEAF] = th
        low[own, 2 * LEAF :] = tl

        def update(j, unused):
            cols = pl.ds(pl.multiple_of(j * LEAF, LEAF), LEAF)
            rh, rl = halves(a[own, cols])
            u = dot(w3, jnp.concatenate([rh, rl, rh], axis=0))
            uh, ul = halves(u)
            a[own, cols] = jnp.zeros((LEAF, LEAF), F32)
            a[:, cols] = a[:, cols] - dot(low[...], jnp.concatenate([uh, ul, uh], axis=0))
            return unused

        lax.fori_loop(k + 1, count, update, 0)
        return unused

    lax.fori_loop(0, count, step, 0)

    def finish(k, unused):
        own = pl.ds(pl.multiple_of(k * LEAF, LEAF), LEAF)
        row = lax.broadcasted_iota(jnp.int32, (PANEL, LEAF), 0)
        value = jnp.where(row < (k + 1) * LEAF, a[:, own], 0.0)
        high, lo = halves(value)
        xh_ref[:, own] = high
        xl_ref[:, own] = lo
        return unused

    lax.fori_loop(0, count, finish, 0)


def chain(panel, extras):
    vmem = pl.BlockSpec(memory_space=pltpu.VMEM)
    return pl.pallas_call(
        chain_kernel,
        out_shape=(
            jax.ShapeDtypeStruct((PANEL, PANEL), BF16),
            jax.ShapeDtypeStruct((PANEL, PANEL), BF16),
            jax.ShapeDtypeStruct((1, PANEL), F32),
        ),
        in_specs=[vmem, vmem],
        out_specs=(vmem, vmem, vmem),
        scratch_shapes=[
            pltpu.VMEM((PANEL, PANEL), F32),
            pltpu.VMEM((LEAF, LEAF), F32),
            pltpu.VMEM((PANEL, 3 * LEAF), BF16),
            pltpu.VMEM((PANEL, 128), F32),
        ],
        compiler_params=pltpu.CompilerParams(vmem_limit_bytes=60 << 20),
        cost_estimate=pl.CostEstimate(flops=100_000_000_000, bytes_accessed=10_000_000, transcendentals=0),
        name="panel_chain",
    )(panel, extras)


def trail_kernel(
    block_ref, own_ref, v1_ref, v2_ref, v3_ref, panel_ref, xh_ref, xl_ref, psq_ref, pextra_ref, extra_ref,
    trail_ref, factor_ref, rows, sq_col, sq_row, kh, kl, fh, fl, vh, vl,
):
    me = lax.axis_index("row")
    slot = lax.axis_index("col")
    row_count = lax.axis_size("row")
    total = 1024 + 3 * LEAF
    rows[0:1024, :] = block_ref[...]
    for s, ref in enumerate((v1_ref, v2_ref, v3_ref)):
        rows[1024 + s * LEAF : 1024 + (s + 1) * LEAF, :] = ref[...]

    def squares(i, unused):
        at = pl.ds(pl.multiple_of(i * LEAF, LEAF), LEAF)
        v = rows[at, :].astype(F32)
        s = jnp.sum(v * v, axis=1, keepdims=True)
        sq_col[at, :] = jnp.broadcast_to(s, (LEAF, 128))
        return unused

    lax.fori_loop(0, total // LEAF, squares, 0)
    own = pl.ds(pl.multiple_of(slot * LEAF, LEAF), LEAF)
    sq_row[0:1, 0:128] = sq_col[own, :].T[0:1, :]
    for s in range(3):
        sq_row[0:1, (s + 1) * LEAF : (s + 2) * LEAF] = sq_col[1024 + s * LEAF : 1024 + (s + 1) * LEAF, :].T[0:1, :]

    lead_row = lax.broadcasted_iota(jnp.int32, (32, 256), 0)
    lead_lane = lax.broadcasted_iota(jnp.int32, (32, 256), 1)

    def kernel_part(n, unused):
        cols = pl.ds(pl.multiple_of(n * 256, 256), 256)
        g = dot_nt(rows[...], panel_ref[cols, :])
        s = sq_col[...]
        k = jnp.exp(-0.5 * (jnp.concatenate([s, s], axis=1) + psq_ref[0:1, cols] - 2.0 * g))
        high, lo = halves(k)
        kh[:, cols] = high
        kl[:, cols] = lo
        extra = pextra_ref[0:1, cols]

        def fix(start, block, scale):
            part = k[start : start + 32, :]
            hit = lead_lane + n * 256 == block * 32 + lead_row
            part = part + jnp.where(hit, extra * scale, 0.0)
            high, lo = halves(part)
            kh[start : start + 32, cols] = high
            kl[start : start + 32, cols] = lo

        fix(0, me, 1.0)
        lead = jnp.where(slot == 0, 1.0, 0.0).astype(F32)
        for s in range(3):
            fix(1024 + s * LEAF, lax.rem(me + row_count - s - 1, row_count), lead)
        return unused

    lax.fori_loop(0, PANEL // 256, kernel_part, 0)
    for n in range(4):
        depth = 256 * (n + 1)
        cols = slice(256 * n, 256 * n + 256)
        f = dot(kh[:, :depth], xh_ref[:depth, cols])
        f = f + dot(kh[:, :depth], xl_ref[:depth, cols])
        f = f + dot(kl[:, :depth], xh_ref[:depth, cols])
        high, lo = halves(f)
        fh[:, cols] = high
        fl[:, cols] = lo
    factor_ref[...] = fh[own, :].astype(F32) + fl[own, :].astype(F32)
    vh[0:LEAF, :] = fh[own, :]
    vl[0:LEAF, :] = fl[own, :]
    vh[LEAF:, :] = fh[1024:, :]
    vl[LEAF:, :] = fl[1024:, :]
    r = lax.broadcasted_iota(jnp.int32, (256, LEAF), 0)
    c = lax.broadcasted_iota(jnp.int32, (256, LEAF), 1)

    def tile(i, unused):
        at = pl.ds(pl.multiple_of(i * 256, 256), 256)
        left = rows[at, :]
        g = jnp.concatenate([dot_nt(left, rows[own, :]), dot_nt(left, rows[1024:, :])], axis=1)
        s = sq_col[at, :]
        k = jnp.exp(-0.5 * (jnp.concatenate([s] * 4, axis=1) + sq_row[...] - 2.0 * g))
        ff = dot_nt(fh[at, :], vh[...])
        ff = ff + dot_nt(fh[at, :], vl[...])
        ff = ff + dot_nt(fl[at, :], vh[...])
        t = k - ff
        trail_ref[at, :] = t
        diagonal = jnp.where(r + i * 256 == c + slot * LEAF, extra_ref[0:1, :], 0.0)
        trail_ref[at, 0:LEAF] = t[:, 0:LEAF] + diagonal
        return unused

    lax.fori_loop(0, 4, tile, 0)


def trail(block, own, visitors, panel, xh, xl, psq, pextra, extra):
    vmem = pl.BlockSpec(memory_space=pltpu.VMEM)
    total = 1024 + 3 * LEAF
    return pl.pallas_call(
        trail_kernel,
        out_shape=(
            jax.ShapeDtypeStruct((1024, STOPS * LEAF), F32),
            jax.ShapeDtypeStruct((LEAF, PANEL), F32),
        ),
        in_specs=[vmem] * 11,
        out_specs=(vmem, vmem),
        scratch_shapes=[
            pltpu.VMEM((total, 2048), BF16),
            pltpu.VMEM((total, 128), F32),
            pltpu.VMEM((1, STOPS * LEAF), F32),
            pltpu.VMEM((total, PANEL), BF16),
            pltpu.VMEM((total, PANEL), BF16),
            pltpu.VMEM((total, PANEL), BF16),
            pltpu.VMEM((total, PANEL), BF16),
            pltpu.VMEM((STOPS * LEAF, PANEL), BF16),
            pltpu.VMEM((STOPS * LEAF, PANEL), BF16),
        ],
        compiler_params=pltpu.CompilerParams(vmem_limit_bytes=60 << 20),
        cost_estimate=pl.CostEstimate(flops=30_000_000_000, bytes_accessed=20_000_000, transcendentals=0),
        name="trailing",
    )(block, own, *visitors, panel, xh, xl, psq, pextra, extra)


def body(embeddings, inverse_scales, matches):
    row_count = lax.axis_size("row")
    share = PANEL // row_count
    scaled = (embeddings.astype(F32) * inverse_scales[None, :]).astype(BF16)
    pairs = matches.reshape(-1, 128, 2).transpose(0, 2, 1).reshape(-1, 128)
    counts = match_counts(pairs)
    extra = 0.1 + 0.5 * counts
    c0 = counts[0, :share].astype(jnp.int32)
    digits = jnp.stack([c0 % 256, (c0 // 256) % 256, c0 // 65536], axis=1).astype(F32).astype(BF16)
    digits = jnp.pad(digits, ((0, 0), (0, 125)))
    lead = jnp.concatenate([scaled[:share], digits], axis=1)
    lead = lax.all_gather(lead, "col")[0]
    panel = lax.all_gather(lead, "row", axis=0, tiled=True)
    d = panel[:, 2048:2051].astype(F32)
    panel_extra = (0.1 + 0.5 * (d[:, 0] + 256.0 * d[:, 1] + 65536.0 * d[:, 2]))[None, :]
    panel = panel[:, :2048]
    block = lax.all_gather(scaled, "col", axis=0, tiled=True)
    visitors = [
        lax.ppermute(scaled, "row", [((i - s) % row_count, i) for i in range(row_count)])
        for s in range(1, STOPS)
    ]
    xh, xl, psq = chain(panel, panel_extra)
    return trail(block, scaled, visitors, panel, xh, xl, psq, panel_extra, extra)


def solution(mesh):
    return jax.shard_map(
        body,
        mesh=mesh,
        in_specs=(P(("row", "col"), None), P(), P()),
        out_specs=(P("row", "col"), P(("row", "col"), None)),
        check_vma=False,
    )
```

time: 608 us -> 221 us (0.36); the launches traced: 597 us -> 220 us
  other arithmetic: 289 us -> 6.63 us
  Pallas kernels: 0 us -> 90.9 us
  local copies, waits for them, and re-layouts: 84.2 us -> 7.56 us
  matrix products: 65.9 us -> 0 us
  waiting for transfers between devices: 130 us -> 93.8 us
    another operation x33 -> x0, other arithmetic: 256 us -> none  [the longest x30 173 us: body(): lower = jnp.linalg.cholesky(diagonal)]
    pallas_call x0 -> x3, Pallas kernels: none -> 90.9 us  [the longest x1 54.2 us: chain(): pl.pallas_call(chain_kernel, out_shape=(jax.ShapeDtypeStruct((PANEL, PANE...]
    squeeze x64 -> x0, local copies, waits for them, and re-layouts: 45 us -> none  [match_counts(): lax.scan(accumulate, jnp.zeros(identity.shape, jnp.float32), grouped)]
    another operation x29 -> x0, matrix products: 36.2 us -> none  [the longest x14 23.1 us: body(): lower = jnp.linalg.cholesky(diagonal)]
    ppermute x6 -> x3, waiting for transfers between devices: 31.6 us -> 0.01 us  [body(): lax.ppermute(scaled, 'row', [((i - s) % row_count, i) for i in range(row_...]
    dot_general x10 -> x0, matrix products: 29.7 us -> none  [the longest x6 15.9 us: kernel_block(): inner = jnp.dot(left, right.T, preferred_element_type=jnp.float32)]
    reduce_sum x70 -> x0, other arithmetic: 26.6 us -> none  [the longest x64 17.7 us: accumulate(): return (carry + jnp.sum(hits, axis=0), None)]
    another operation x33 -> x0, local copies, waits for them, and re-layouts: 25.6 us -> none
  transfers between devices with their start and end apart: 10 -> 6, of which waited for: 9 -> 2; matrix products, arithmetic and copies ran while one was open for 15% -> 4% of each run, Pallas kernels for 0% -> 25%
where the time goes in v1:
time: 221 us; the launch traced here: 220 us
  waiting for transfers between devices  93.8 us (42%)
  Pallas kernels  90.9 us (41%)
  between operations  13.8 us (6%)
  starting transfers between devices  7.64 us (3%)
  local copies, waits for them, and re-layouts  7.56 us (3%)
  other arithmetic  6.63 us (3%)
    all_gather x1, waiting for transfers between devices, body(): panel = lax.all_gather(lead, 'row', axis=0, tiled=True)  55 us
    pallas_call x1, Pallas kernels, chain(): pl.pallas_call(chain_kernel, out_shape=(jax.ShapeDtypeStruct((PANEL, PANE...  54.2 us
    all_gather x1, waiting for transfers between devices, body(): lead = lax.all_gather(lead, 'col')[0]  38.8 us
    pallas_call x1, Pallas kernels, trail(): pl.pallas_call(trail_kernel, out_shape=(jax.ShapeDtypeStruct((1024, STOPS...  30.5 us
    ppermute x3, starting transfers between devices, body(): lax.ppermute(scaled, 'row', [((i - s) % row_count, i) for i in range(row_...  7.51 us
    pallas_call x1, Pallas kernels, match_counts(): pl.pallas_call(functools.partial(count_kernel, base), out_shape=jax.Shape...  6.25 us
    slice x1, local copies, waits for them, and re-layouts, body(): panel = panel[:, :2048]  4.8 us
  transfers between devices with their start and end apart: 6, of which 2 were waited for; matrix products, arithmetic and copies ran while one was open for 4% of the time, Pallas kernels for 25%

profile of v1, /device:TPU:1, one launch (start us, length us, event | category | flops | bytes accessed | tf_op | source)
XLA Modules:
  0.0 220.4 jit_solution(5432837321107181984)
XLA Ops:
  7.2 0.0 all-gather.9.cloned.1.call-start
  7.2 6.3 %match_counts.1 = f32[8,128]{1,0:T(8,128)} custom-call(s32[512,128]{1,0:T(8,128)} %bitcast.29), custom_call_target="tpu_custom_call" | custom-call | tf_op jit(solution)/shard_map/match_counts/pallas_call | solution.py:83
  13.5 0.7 and_select_fusion.3
  14.2 0.7 and_select_fusion.1
  14.9 0.1 copy.18
  15.0 1.1 multiply_convert_fusion.own_ref
  16.1 0.0 copy-start
  16.2 0.7 fusion.6
  16.9 0.0 all-gather.9.cloned.1.call-update
  16.9 0.0 all-gather.11.cloned.1.call-start
  17.0 38.8 %all-gather.9.cloned.1.call-done = bf16[256,2176]{1,0:T(8,128)(2,1)} async-done(((bf16[32,2176]{1,0:T(8,128)(2,1)}), bf16[256,2176]{1,0:T(8,128)(2,1)}) %all-gather.9.cloned.1.call-update) | async-done | bytes 1114128 | tf_op jit(solution)/shard_map/all_gather | solution.py:324
  55.7 1.6 slice.34
  57.3 0.0 all-gather.11.cloned.1.call-update
  57.3 0.0 all-gather.7.cloned.1.call-start
  57.4 7.2 %collective-permute-start.2 = (bf16[128,2048]{1,0:T(8,128)(2,1)S(1)}, bf16[128,2048]{1,0:T(8,128)(2,1)S(1)}, u32[]{:S(2)}, u32[]{:S(2)}) collective-permute-start(bf16[128,2048]{1,0:T(8,128)(2,1)S(1)} %multiply_convert_fusion.own_ref), channel_id=1, source_target_pairs={{232,0},{240,8},{248,16},{0,24},{8,32},{16,40},{24,48},{32,56},{40... | collective-permute-start | bytes 1572872 | tf_op jit(solution)/shard_map/ppermute | solution.py:331
  64.6 0.3 collective-permute-start.1
  64.9 0.0 collective-permute-start
  64.9 0.0 all-gather.7.cloned.1.call-update
  64.9 1.3 multiply_add_fusion.extra_ref
  66.2 55.0 %all-gather.11.cloned.1.call-done = bf16[1024,2176]{1,0:T(8,128)(2,1)} async-done(((bf16[32,2176]{1,0:T(8,128)(2,1)}), bf16[1024,2176]{1,0:T(8,128)(2,1)}) %all-gather.11.cloned.1.call-update) | async-done | bytes 4456464 | tf_op jit(solution)/shard_map/all_gather | solution.py:325
  121.2 1.0 slice_convert_fusion
  122.2 1.1 fusion.3
  123.3 4.8 %slice.35.panel_ref = bf16[1024,2048]{1,0:T(8,128)(2,1)} slice(bf16[1024,2176]{1,0:T(8,128)(2,1)} %all-gather.11.cloned.1.call-done), slice={[0:1024], [0:2048]} | slice | bytes 8388608 | tf_op jit(solution)/shard_map/slice | solution.py:328
  128.1 54.2 %panel_chain.1 = (bf16[1024,1024]{1,0:T(8,128)(2,1)}, bf16[1024,1024]{1,0:T(8,128)(2,1)}, f32[1,1024]{1,0:T(1,128)}) custom-call(bf16[1024,2048]{1,0:T(8,128)(2,1)} %slice.35.panel_ref, f32[1,1024]{1,0:T(1,128)} %bitcast.30), custom_call_target="tpu_custom_call" | custom-call | flops 99999997952 | bytes 10000000 | tf_op jit(solution)/shard_map/panel_chain/pallas_call | solution.py:176
  182.2 0.0 collective-permute-done.2.v3_ref
  182.2 0.0 collective-permute-done.1.v2_ref
  182.2 0.0 collective-permute-done.v1_ref
  182.3 0.0 all-gather.7.cloned.1.call-done.block_ref
  182.3 0.7 copy-done.1
  183.0 0.2 copy-done.2
  183.2 0.1 copy-done.3
  183.4 30.5 %trailing.1 = (f32[1024,512]{1,0:T(8,128)}, f32[128,1024]{1,0:T(8,128)}) custom-call(bf16[1024,2048]{1,0:T(8,128)(2,1)} %all-gather.7.cloned.1.call-done.block_ref, bf16[128,2048]{1,0:T(8,128)(2,1)} %copy-done, bf16[128,2048]{1,0:T(8,128)(2,1)} %copy-done.3, bf16[128,2048]{1,0:T(8,128)(2,1)} %copy-done.2, bf16[128,2048]{1,0:T(8,128)(2,1)} %copy-done.1, ...), custom_call_target="tpu_custom_call" | custom-call | flops 30000001024 | bytes 20000000 | tf_op jit(solution)/shard_map/trailing/pallas_call | solution.py:288
  (6 shorter events, 0.0 us)
Async XLA Ops:
  7.2 48.6 %all-gather.9.cloned.1.call-start = ((), (), s32[]{:S(2)}) async-start(), calls=%async_computation.1 | async-start | bytes 1253376 | tf_op jit(solution)/shard_map/all_gather | solution.py:324
  16.1 48.8 %copy-start = (bf16[128,2048]{1,0:T(8,128)(2,1)}, bf16[128,2048]{1,0:T(8,128)(2,1)S(1)}, u32[]{:S(2)}) copy-start(bf16[128,2048]{1,0:T(8,128)(2,1)S(1)} %multiply_convert_fusion.own_ref) | copy-start | bytes 1572868
  16.9 104.3 %all-gather.11.cloned.1.call-start = ((), (), s32[]{:S(2)}) async-start(), calls=%async_computation.2 | async-start | bytes 4595712 | tf_op jit(solution)/shard_map/all_gather | solution.py:325
  57.3 125.0 %all-gather.7.cloned.1.call-start = ((), (), s32[]{:S(2)}) async-start(), calls=%async_computation | async-start | bytes 4718592 | tf_op jit(solution)/shard_map/all_gather | solution.py:329
  57.4 124.8 %collective-permute-start.2 = (bf16[128,2048]{1,0:T(8,128)(2,1)S(1)}, bf16[128,2048]{1,0:T(8,128)(2,1)S(1)}, u32[]{:S(2)}, u32[]{:S(2)}) collective-permute-start(bf16[128,2048]{1,0:T(8,128)(2,1)S(1)} %multiply_convert_fusion.own_ref), channel_id=1, source_target_pairs={{232,0},{240,8},{248,16},{0,24},{8,32},{16,40},{24,48},{32,56},{40... | collective-permute-start | bytes 1572872 | tf_op jit(solution)/shard_map/ppermute | solution.py:331
  64.6 117.6 %collective-permute-start.1 = (bf16[128,2048]{1,0:T(8,128)(2,1)S(1)}, bf16[128,2048]{1,0:T(8,128)(2,1)S(1)}, u32[]{:S(2)}, u32[]{:S(2)}) collective-permute-start(bf16[128,2048]{1,0:T(8,128)(2,1)S(1)} %multiply_convert_fusion.own_ref), channel_id=1, source_target_pairs={{240,0},{248,8},{0,16},{8,24},{16,32},{24,40},{32,48},{40,56},{48,... | collective-permute-start | bytes 1572872 | tf_op jit(solution)/shard_map/ppermute | solution.py:331
  64.9 117.3 %collective-permute-start = (bf16[128,2048]{1,0:T(8,128)(2,1)S(1)}, bf16[128,2048]{1,0:T(8,128)(2,1)S(1)}, u32[]{:S(2)}, u32[]{:S(2)}) collective-permute-start(bf16[128,2048]{1,0:T(8,128)(2,1)S(1)} %multiply_convert_fusion.own_ref), channel_id=1, source_target_pairs={{248,0},{0,8},{8,16},{16,24},{24,32},{32,40},{40,48},{48,56},{56,6... | collective-permute-start | bytes 1572872 | tf_op jit(solution)/shard_map/ppermute | solution.py:331
  182.2 0.8 copy-start.1
  182.2 1.0 copy-start.2
  182.3 1.1 copy-start.3
Sparse Core Ops, SparseCore 0:
  17.0 38.6 all-gather.8
  58.8 62.2 all-gather.10
  123.0 53.8 all-gather.6

commit v2 on v1

--- a/solution.py
+++ b/solution.py
@@ -58,44 +58,231 @@
             rows[i] = jnp.where(lane == k, 0.0, rows[i]) - c[i] * u
 
 
-def count_kernel(base, matches_ref, out_ref, hits):
-    first = base()
-
-    def step(i, unused):
-        ids = [first + 4 * i + q for q in range(4)]
-        totals = [jnp.zeros((8, 128), F32) for q in range(4)]
-        for block in range(matches_ref.shape[0] // 8):
-            values = matches_ref[8 * block : 8 * block + 8, :]
-            for q in range(4):
-                totals[q] = totals[q] + jnp.where(values == ids[q], 1.0, 0.0)
-        for q in range(4):
-            hits[pl.ds(4 * i + q, 1), :] = jnp.sum(totals[q], axis=0, keepdims=True)
-        return unused
-
-    lax.fori_loop(0, 32, step, 0)
-    out_ref[...] = jnp.broadcast_to(jnp.sum(hits[...].T, axis=0, keepdims=True), (8, 128))
-
-
-def match_counts(matches):
-    def base():
-        return (lax.axis_index("row") * lax.axis_size("col") + lax.axis_index("col")) * LEAF
-
+MESH = pl.DeviceIdType.MESH
+SIDE = 4
+
+
+def counts_step(values, first):
+    sub32 = lax.broadcasted_iota(jnp.int32, (32, 128), 0)
+    sub16 = lax.broadcasted_iota(jnp.int32, (16, 128), 0)
+    place = jnp.where((values & 1023) < 32, values & 31, -1)
+    inside = values - first
+    part = jnp.where((inside >= 0) & (inside < 128), inside >> 4, -1)
+    left = jnp.concatenate(
+        [jnp.where(sub32 == values >> 10, 1.0, 0.0), jnp.where(sub16 == part, 1.0, 0.0)], axis=0
+    ).astype(BF16)
+    right = jnp.concatenate(
+        [jnp.where(sub32 == place, 1.0, 0.0), jnp.where(sub16 == (values & 15), 1.0, 0.0)], axis=0
+    ).astype(BF16)
+    return left, right
+
+
+def spread(table, width):
+    n = table.shape[0]
+    total = n * width
+    tiled = jnp.concatenate([table] * n, axis=1)
+    row = lax.broadcasted_iota(jnp.int32, (n, total), 0)
+    lane = lax.broadcasted_iota(jnp.int32, (n, total), 1)
+    return jnp.sum(jnp.where(lane >> (width.bit_length() - 1) == row, tiled, 0.0), axis=0, keepdims=True)
+
+
+def gather_kernel(
+    emb_ref, inv_ref, pairs_ref, scaled_ref, panel, pextra_ref, extra_ref, hits, zs, zr, ss, sr, cs, cr,
+):
+    me = lax.axis_index("row")
+    slot = lax.axis_index("col")
+    x, y, core = me // 8, (me // 2) % SIDE, me % 2
+    xp, xm, xo = (x + 1) % SIDE, (x + 3) % SIDE, (x + 2) % SIDE
+    yp, ym, yo = (y + 1) % SIDE, (y + 3) % SIDE, (y + 2) % SIDE
+
+    def row_at(x, y, core):
+        return (x * SIDE + y) * 2 + core
+
+    to_xp, to_xm = row_at(xp, y, core), row_at(xm, y, core)
+    to_yp, to_ym = row_at(x, yp, core), row_at(x, ym, core)
+    twin = row_at(x, y, 1 - core)
+    barrier = pltpu.get_barrier_semaphore()
+    for other in (to_xp, to_xm, to_yp, to_ym, twin):
+        pl.semaphore_signal(barrier, inc=1, device_id=(other, slot), device_id_type=MESH)
+    for j in range(1, 8):
+        pl.semaphore_signal(barrier, inc=1, device_id=(me, (slot + j) % 8), device_id_type=MESH)
+
+    def scale(start, count):
+        v = emb_ref[start : start + count, :].astype(F32) * inv_ref[0:1, :]
+        scaled_ref[start : start + count, :] = v.astype(BF16)
+
+    scale(0, 32)
+
+    @pl.when(slot == 0)
+    def _():
+        panel[x, y, core] = scaled_ref[0:32, :]
+
+    pl.semaphore_wait(barrier, 12)
+
+    def copy(view, row, col, send, recv):
+        return pltpu.make_async_remote_copy(
+            src_ref=view, dst_ref=view, send_sem=send, recv_sem=recv, device_id=(row, col), device_id_type=MESH
+        )
+
+    def chunk(q):
+        return panel.at[x, y, core, :, pl.ds(pl.multiple_of(q * 256, 256), 256)]
+
+    @pl.when(slot == 0)
+    def _():
+        for c in range(1, 8):
+            copy(chunk(c), me, c, zs.at[c], zr.at[c]).start()
+        for c in range(1, 8):
+            copy(chunk(0), me, c, zs.at[7 + c], zr.at[0]).start()
+
+    scale(32, 96)
+
+    @pl.when(slot != 0)
+    def _():
+        copy(chunk(slot), me, slot, zs.at[0], zr.at[slot]).wait_recv()
+        for j in range(1, 8):
+            other = (slot + j) % 8
+
+            @pl.when(other != 0)
+            def _(other=other, j=j):
+                copy(chunk(slot), me, other, zs.at[j], zr.at[slot]).start()
+
+    first = row_at(x, y, core) * 1024 + slot * 128
+
+    def count(i, total):
+        lefts, rights = [], []
+        for r in range(8):
+            left, right = counts_step(jnp.broadcast_to(pairs_ref[pl.ds(i * 8 + r, 1), :], (8, 128))[0:1, :], first)
+            lefts.append(left)
+            rights.append(right)
+        return total + dot_nt(jnp.concatenate(lefts, axis=1), jnp.concatenate(rights, axis=1))
+
+    hits[:, 0:48] = lax.fori_loop(0, pairs_ref.shape[0] // 8, count, jnp.zeros((48, 48), F32))
+
+    @pl.when(slot != 0)
+    def _():
+        for j in range(1, 8):
+            other = (slot + j) % 8
+            copy(chunk(other), me, slot, zs.at[0], zr.at[other]).wait_recv()
+
+    near, far = pl.ds(0, 1024), pl.ds(1024, 1024)
+    sent = []
+
+    def send(view, row, i):
+        c = copy(view, row, slot, ss.at[i], sr.at[i])
+        c.start()
+        sent.append(c)
+
+    def arrive(view, i):
+        copy(view, twin, slot, ss.at[i], sr.at[i]).wait_recv()
+
+    passed = []
+
+    def share(view, back, i):
+        c = copy(view, twin, slot, cs.at[i], cr.at[i])
+        c.start()
+        passed.append((c, back, i))
+
+    own_near, own_far = panel.at[x, y, core, :, near], panel.at[x, y, core, :, far]
+    send(own_near, to_xp, 0)
+    send(own_far, to_yp, 1)
+    send(own_near, to_xm, 2)
+    send(own_far, to_ym, 3)
+    share(panel.at[x, y, core], panel.at[x, y, 1 - core], 0)
+    top, low = pl.ds(0, 16), pl.ds(16, 16)
+    arrive(panel.at[xm, y, core, :, near], 0)
+    send(panel.at[xm, y, core, top, near], to_xp, 4)
+    arrive(panel.at[x, ym, core, :, far], 1)
+    send(panel.at[x, ym, core, top, far], to_yp, 5)
+    arrive(panel.at[xp, y, core, :, near], 2)
+    send(panel.at[xp, y, core, low, near], to_xm, 6)
+    arrive(panel.at[x, yp, core, :, far], 3)
+    send(panel.at[x, yp, core, low, far], to_ym, 7)
+    share(panel.at[xm, y, core, :, near], panel.at[xm, y, 1 - core, :, near], 1)
+    share(panel.at[x, ym, core, :, far], panel.at[x, ym, 1 - core, :, far], 2)
+    share(panel.at[xp, y, core, :, near], panel.at[xp, y, 1 - core, :, near], 3)
+    share(panel.at[x, yp, core, :, far], panel.at[x, yp, 1 - core, :, far], 4)
+    arrive(panel.at[xo, y, core, top, near], 4)
+    arrive(panel.at[xo, y, core, low, near], 6)
+    send(panel.at[:, y, core, :, near], to_yp, 8)
+    send(panel.at[:, y, core, :, near], to_ym, 10)
+    arrive(panel.at[x, yo, core, top, far], 5)
+    arrive(panel.at[x, yo, core, low, far], 7)
+    send(panel.at[x, :, core, :, far], to_xp, 9)
+    send(panel.at[x, :, core, :, far], to_xm, 11)
+    share(panel.at[xo, y, core, :, near], panel.at[xo, y, 1 - core, :, near], 5)
+    share(panel.at[x, yo, core, :, far], panel.at[x, yo, 1 - core, :, far], 6)
+
+    row_hits = hits[:, 0:48]
+    pextra_ref[...] = 0.1 + 0.5 * spread(row_hits[0:32, 0:32], 32)
+    extra_ref[...] = 0.1 + 0.5 * spread(row_hits[32:40, 32:48], 16)
+
+    first_two, last_two = pl.ds(0, 2), pl.ds(2, 2)
+    arrive(panel.at[:, ym, core, :, near], 8)
+    send(panel.at[first_two, ym, core, :, near], to_yp, 12)
+    arrive(panel.at[xm, :, core, :, far], 9)
+    send(panel.at[xm, first_two, core, :, far], to_xp, 13)
+    arrive(panel.at[:, yp, core, :, near], 10)
+    send(panel.at[last_two, yp, core, :, near], to_ym, 14)
+    arrive(panel.at[xp, :, core, :, far], 11)
+    send(panel.at[xp, last_two, core, :, far], to_xm, 15)
+    share(panel.at[:, ym, core, :, near], panel.at[:, ym, 1 - core, :, near], 7)
+    share(panel.at[xm, :, core, :, far], panel.at[xm, :, 1 - core, :, far], 8)
+    share(panel.at[:, yp, core, :, near], panel.at[:, yp, 1 - core, :, near], 9)
+    share(panel.at[xp, :, core, :, far], panel.at[xp, :, 1 - core, :, far], 10)
+    arrive(panel.at[first_two, yo, core, :, near], 12)
+    arrive(panel.at[last_two, yo, core, :, near], 14)
+    share(panel.at[:, yo, core, :, near], panel.at[:, yo, 1 - core, :, near], 11)
+    arrive(panel.at[xo, first_two, core, :, far], 13)
+    arrive(panel.at[xo, last_two, core, :, far], 15)
+    share(panel.at[xo, :, core, :, far], panel.at[xo, :, 1 - core, :, far], 12)
+    for c, back, i in passed:
+        copy(back, twin, slot, cs.at[i], cr.at[i]).wait_recv()
+        c.wait_send()
+    for c in sent:
+        c.wait_send()
+
+    @pl.when(slot == 0)
+    def _():
+        for c in range(1, 8):
+            copy(chunk(c), me, c, zs.at[c], zr.at[c]).wait_send()
+            copy(chunk(0), me, c, zs.at[7 + c], zr.at[0]).wait_send()
+
+    @pl.when(slot != 0)
+    def _():
+        for j in range(1, 8):
+            other = (slot + j) % 8
+
+            @pl.when(other != 0)
+            def _(other=other, j=j):
+                copy(chunk(slot), me, other, zs.at[j], zr.at[slot]).wait_send()
+
+
+def gather_panel(embeddings, inverse_scales, pairs):
+    vmem = pl.BlockSpec(memory_space=pltpu.VMEM)
     return pl.pallas_call(
-        functools.partial(count_kernel, base),
-        out_shape=jax.ShapeDtypeStruct((8, 128), F32),
-        in_specs=[pl.BlockSpec(memory_space=pltpu.VMEM)],
-        out_specs=pl.BlockSpec(memory_space=pltpu.VMEM),
-        scratch_shapes=[pltpu.VMEM((128, 128), F32)],
-        name="match_counts",
-    )(matches)
-
-
-def squares_column(x_ref, start, count, chunk=128):
-    parts = []
-    for i in range(count // chunk):
-        v = x_ref[start + i * chunk : start + (i + 1) * chunk, :].astype(F32)
-        parts.append(jnp.sum(v * v, axis=1, keepdims=True))
-    return parts
+        gather_kernel,
+        out_shape=(
+            jax.ShapeDtypeStruct((LEAF, 2048), BF16),
+            jax.ShapeDtypeStruct((SIDE, SIDE, 2, 32, 2048), BF16),
+            jax.ShapeDtypeStruct((1, PANEL), F32),
+            jax.ShapeDtypeStruct((1, LEAF), F32),
+        ),
+        in_specs=[vmem] * 3,
+        out_specs=(vmem,) * 4,
+        scratch_shapes=[
+            pltpu.VMEM((48, 128), F32),
+            pltpu.SemaphoreType.DMA((15,)),
+            pltpu.SemaphoreType.DMA((8,)),
+            pltpu.SemaphoreType.DMA((16,)),
+            pltpu.SemaphoreType.DMA((16,)),
+            pltpu.SemaphoreType.DMA((13,)),
+            pltpu.SemaphoreType.DMA((13,)),
+        ],
+        compiler_params=pltpu.CompilerParams(
+            collective_id=0, has_side_effects=True, vmem_limit_bytes=40 << 20
+        ),
+        name="panel_gather",
+    )(embeddings, inverse_scales, pairs)
 
 
 def to_lanes(column):
@@ -312,20 +499,9 @@
 
 def body(embeddings, inverse_scales, matches):
     row_count = lax.axis_size("row")
-    share = PANEL // row_count
-    scaled = (embeddings.astype(F32) * inverse_scales[None, :]).astype(BF16)
     pairs = matches.reshape(-1, 128, 2).transpose(0, 2, 1).reshape(-1, 128)
-    counts = match_counts(pairs)
-    extra = 0.1 + 0.5 * counts
-    c0 = counts[0, :share].astype(jnp.int32)
-    digits = jnp.stack([c0 % 256, (c0 // 256) % 256, c0 // 65536], axis=1).astype(F32).astype(BF16)
-    digits = jnp.pad(digits, ((0, 0), (0, 125)))
-    lead = jnp.concatenate([scaled[:share], digits], axis=1)
-    lead = lax.all_gather(lead, "col")[0]
-    panel = lax.all_gather(lead, "row", axis=0, tiled=True)
-    d = panel[:, 2048:2051].astype(F32)
-    panel_extra = (0.1 + 0.5 * (d[:, 0] + 256.0 * d[:, 1] + 65536.0 * d[:, 2]))[None, :]
-    panel = panel[:, :2048]
+    scaled, panel, panel_extra, extra = gather_panel(embeddings, inverse_scales[None, :], pairs)
+    panel = panel.reshape(PANEL, -1)
     block = lax.all_gather(scaled, "col", axis=0, tiled=True)
     visitors = [
         lax.ppermute(scaled, "row", [((i - s) % row_count, i) for i in range(row_count)])

time: 221 us -> 155 us (0.70)
  waiting for transfers between devices: 93.8 us -> 0.05 us
  Pallas kernels: 90.9 us -> 129 us
  other arithmetic: 6.63 us -> 0 us
  starting transfers between devices: 7.64 us -> 2.39 us
    all_gather x2 -> x0, waiting for transfers between devices: 93.7 us -> none  [the longest x1 55 us: body(): panel = lax.all_gather(lead, 'row', axis=0, tiled=True)]
    pallas_call x1, Pallas kernels: 6.25 us -> 44.5 us  [gather_panel(): pl.pallas_call(gather_kernel, out_shape=(jax.ShapeDtypeStruct((LEAF, 2048...]
    slice x3 -> x0, local copies, waits for them, and re-layouts: 6.38 us -> none  [the longest x1 4.8 us: body(): panel = panel[:, :2048]]
    unnamed x8 -> x18, local copies, waits for them, and re-layouts: 1.08 us -> 6.93 us
    ppermute x3, starting transfers between devices: 7.51 us -> 2.35 us  [body(): lax.ppermute(scaled, 'row', [((i - s) % row_count, i) for i in range(row_...]
    add x2 -> x0, other arithmetic: 2.37 us -> none  [the longest x1 1.28 us: body(): extra = 0.1 + 0.5 * counts]
  transfers between devices with their start and end apart: 6 -> 4, of which waited for: 2 -> 0; matrix products, arithmetic and copies ran while one was open for 4% -> 0% of each run, Pallas kernels for 25% -> 35%
where the time goes in v2:
time: 155 us; the launch traced here: 153 us
  Pallas kernels  129 us (83%)
  between operations  14.1 us (9%)
  local copies, waits for them, and re-layouts  6.93 us (4%)
  starting transfers between devices  2.39 us (2%)
    pallas_call x1, Pallas kernels, chain(): pl.pallas_call(chain_kernel, out_shape=(jax.ShapeDtypeStruct((PANEL, PANE...  54.1 us
    pallas_call x1, Pallas kernels, gather_panel(): pl.pallas_call(gather_kernel, out_shape=(jax.ShapeDtypeStruct((LEAF, 2048...  44.5 us
    pallas_call x1, Pallas kernels, trail(): pl.pallas_call(trail_kernel, out_shape=(jax.ShapeDtypeStruct((1024, STOPS...  30.5 us
    unnamed x18, local copies, waits for them, and re-layouts  6.93 us
  transfers between devices with their start and end apart: 4, of which 0 were waited for; matrix products, arithmetic and copies ran while one was open for 0% of the time, Pallas kernels for 35%

profile of v2, /device:TPU:1, one launch (start us, length us, event | category | flops | bytes accessed | tf_op | source)
XLA Modules:
  0.0 152.6 jit_solution(16183946155891302195)
XLA Ops:
  7.2 0.0 all-gather.2.cloned.1.call-start
  7.2 0.0 copy-start
  7.2 1.0 copy-done
  8.3 0.0 copy-start.1
  8.3 0.9 copy-done.1
  9.2 0.0 copy-start.2
  9.2 0.7 copy-done.2
  9.9 44.5 %panel_gather.1 = (bf16[128,2048]{1,0:T(8,128)(2,1)}, bf16[4,4,2,32,2048]{4,3,2,1,0:T(8,128)(2,1)S(1)}, f32[1,1024]{1,0:T(1,128)S(1)}, f32[1,128]{1,0:T(1,128)S(1)}) custom-call(bf16[128,2048]{1,0:T(8,128)(2,1)S(1)} %copy-done, f32[1,2048]{1,0:T(1,128)S(1)} %bitcast.8, s32[512,128]{1,0:T(8,128)S(1)} %bitcast.7), custom_call_target="tpu_custom_call" | custom-call | tf_op jit(solution)/shard_map/panel_gather/pallas_call | solution.py:262
  54.4 0.0 copy-start.3
  54.4 2.0 %copy-done.3 = bf16[4,4,2,32,2048]{4,3,2,1,0:T(8,128)(2,1)} copy-done((bf16[4,4,2,32,2048]{4,3,2,1,0:T(8,128)(2,1)}, bf16[4,4,2,32,2048]{4,3,2,1,0:T(8,128)(2,1)S(1)}, u32[]{:S(2)}) %copy-start.3) | copy-done | bytes 4194328
  56.4 0.0 copy-start.4
  56.4 0.6 copy-done.4
  57.0 0.0 copy-start.5
  57.0 0.6 copy-done.5
  57.6 0.0 all-gather.2.cloned.1.call-update
  57.6 1.7 %collective-permute-start.2 = (bf16[128,2048]{1,0:T(8,128)(2,1)}, bf16[128,2048]{1,0:T(8,128)(2,1)S(1)}, u32[]{:S(2)}, u32[]{:S(2)}) collective-permute-start(bf16[128,2048]{1,0:T(8,128)(2,1)} %get-tuple-element.9.own_ref), channel_id=1, source_target_pairs={{232,0},{240,8},{248,16},{0,24},{8,32},{16,40},{24,48},{32,56},{40... | collective-permute-start | bytes 1572872 | tf_op jit(solution)/shard_map/ppermute | solution.py:507
  59.3 0.0 collective-permute-start.1
  59.3 0.6 collective-permute-start
  59.9 54.1 %panel_chain.1 = (bf16[1024,1024]{1,0:T(8,128)(2,1)}, bf16[1024,1024]{1,0:T(8,128)(2,1)}, f32[1,1024]{1,0:T(1,128)}) custom-call(bf16[1024,2048]{1,0:T(8,128)(2,1)} %bitcast.9, f32[1,1024]{1,0:T(1,128)} %copy-done.4), custom_call_target="tpu_custom_call" | custom-call | flops 99999997952 | bytes 10000000 | tf_op jit(solution)/shard_map/panel_chain/pallas_call | solution.py:363
  114.0 0.0 collective-permute-done.2.v3_ref
  114.0 0.0 copy-start.6
  114.0 0.0 collective-permute-done.1.v2_ref
  114.0 0.0 copy-start.7
  114.1 0.0 collective-permute-done.v1_ref
  114.1 0.0 copy-start.8
  114.1 0.0 all-gather.2.cloned.1.call-done.block_ref
  114.1 0.7 copy-done.6
  114.8 0.2 copy-done.7
  115.0 0.2 copy-done.8
  115.2 30.5 %trailing.1 = (f32[1024,512]{1,0:T(8,128)}, f32[128,1024]{1,0:T(8,128)}) custom-call(bf16[1024,2048]{1,0:T(8,128)(2,1)} %all-gather.2.cloned.1.call-done.block_ref, bf16[128,2048]{1,0:T(8,128)(2,1)} %get-tuple-element.9.own_ref, bf16[128,2048]{1,0:T(8,128)(2,1)} %copy-done.8, bf16[128,2048]{1,0:T(8,128)(2,1)} %copy-done.7, bf16[128,2048]{1,0:T(8,128)(2,1)} %copy-done.6, ...), custom_call_target="tpu_custom_call" | custom-call | flops 30000001024 | bytes 20000000 | tf_op jit(solution)/shard_map/trailing/pallas_call | solution.py:475
Async XLA Ops:
  7.2 106.9 %all-gather.2.cloned.1.call-start = ((), (), s32[]{:S(2)}) async-start(), calls=%async_computation | async-start | bytes 4718592 | tf_op jit(solution)/shard_map/all_gather | solution.py:505
  7.2 1.0 copy-start
  8.3 0.9 copy-start.1
  9.2 0.7 copy-start.2
  54.4 2.0 %copy-start.3 = (bf16[4,4,2,32,2048]{4,3,2,1,0:T(8,128)(2,1)}, bf16[4,4,2,32,2048]{4,3,2,1,0:T(8,128)(2,1)S(1)}, u32[]{:S(2)}) copy-start(bf16[4,4,2,32,2048]{4,3,2,1,0:T(8,128)(2,1)S(1)} %get-tuple-element.10) | copy-start | bytes 12582916
  56.4 0.6 copy-start.4
  57.0 0.6 copy-start.5
  57.6 56.4 %collective-permute-start.2 = (bf16[128,2048]{1,0:T(8,128)(2,1)}, bf16[128,2048]{1,0:T(8,128)(2,1)S(1)}, u32[]{:S(2)}, u32[]{:S(2)}) collective-permute-start(bf16[128,2048]{1,0:T(8,128)(2,1)} %get-tuple-element.9.own_ref), channel_id=1, source_target_pairs={{232,0},{240,8},{248,16},{0,24},{8,32},{16,40},{24,48},{32,56},{40... | collective-permute-start | bytes 1572872 | tf_op jit(solution)/shard_map/ppermute | solution.py:507
  59.3 54.7 %collective-permute-start.1 = (bf16[128,2048]{1,0:T(8,128)(2,1)}, bf16[128,2048]{1,0:T(8,128)(2,1)S(1)}, u32[]{:S(2)}, u32[]{:S(2)}) collective-permute-start(bf16[128,2048]{1,0:T(8,128)(2,1)} %get-tuple-element.9.own_ref), channel_id=1, source_target_pairs={{240,0},{248,8},{0,16},{8,24},{16,32},{24,40},{32,48},{40,56},{48,... | collective-permute-start | bytes 1572872 | tf_op jit(solution)/shard_map/ppermute | solution.py:507
  59.3 54.7 %collective-permute-start = (bf16[128,2048]{1,0:T(8,128)(2,1)}, bf16[128,2048]{1,0:T(8,128)(2,1)S(1)}, u32[]{:S(2)}, u32[]{:S(2)}) collective-permute-start(bf16[128,2048]{1,0:T(8,128)(2,1)} %get-tuple-element.9.own_ref), channel_id=1, source_target_pairs={{248,0},{0,8},{8,16},{16,24},{24,32},{32,40},{40,48},{48,56},{56,6... | collective-permute-start | bytes 1572872 | tf_op jit(solution)/shard_map/ppermute | solution.py:507
  114.0 0.8 copy-start.6
  114.0 1.0 copy-start.7
  114.1 1.1 copy-start.8
Sparse Core Ops, SparseCore 0:
  57.7 56.2 all-gather.1

commit v3 on v2

--- a/solution.py
+++ b/solution.py
@@ -289,7 +289,59 @@
     return jnp.broadcast_to(column, (128, 128)).T[0:1, :]
 
 
-def chain_kernel(panel_ref, extra_ref, xh_ref, xl_ref, sq_ref, a, leaf, low, sq_col):
+def chain_steps(a, leaf, low, up):
+    count = PANEL // LEAF
+    r128 = lax.broadcasted_iota(jnp.int32, (LEAF, LEAF), 0)
+    c128 = lax.broadcasted_iota(jnp.int32, (LEAF, LEAF), 1)
+    lane = lax.broadcasted_iota(jnp.int32, (LEAF, PANEL), 1)
+
+    def beside(x):
+        high, lo = halves(x)
+        return jnp.concatenate([high, high, lo], axis=1)
+
+    def above(x):
+        high, lo = halves(x)
+        return jnp.concatenate([high, lo, high], axis=0)
+
+    def inverse():
+        w = jnp.where(r128 >= c128, leaf[...], 0.0)
+        return w, w.T
+
+    def block(k):
+        return pl.ds(pl.multiple_of(k * LEAF, LEAF), LEAF)
+
+    leaf_factor(a[0:LEAF, 0:LEAF], leaf)
+
+    def step(m, unused):
+        own, after = block(m), block(m + 1)
+        w, wt = inverse()
+        w3, t3 = beside(w), above(wt)
+        next_low = dot(beside(a[after, own]), t3)
+        next_up = dot(w3, above(a[own, after]))
+        tile = a[after, after] - dot(beside(next_low), above(next_up))
+        lcol = dot(beside(a[:, own]), t3)
+        a[:, own] = lcol
+        a[own, own] = wt
+        low[...] = beside(lcol)
+        low[own, :] = beside(wt)
+        mine = a[own, :]
+        later = lane >= (m + 1) * LEAF
+        up[...] = above(jnp.where(later, dot(w3, above(mine)), 0.0))
+        a[own, :] = jnp.where(later, 0.0, mine)
+        for n in range(PANEL // 256):
+            cols = slice(256 * n, 256 * n + 256)
+            a[:, cols] = a[:, cols] - dot(low[...], up[:, cols])
+        leaf_factor(tile, leaf)
+        return unused
+
+    lax.fori_loop(0, count - 1, step, 0)
+    last = block(count - 1)
+    w, wt = inverse()
+    a[:, last] = dot(beside(a[:, last]), above(wt))
+    a[last, last] = wt
+
+
+def chain_kernel(panel_ref, extra_ref, xh_ref, xl_ref, sq_ref, a, leaf, low, up, sq_col):
     count = PANEL // LEAF
     for i in range(count):
         v = panel_ref[i * LEAF : (i + 1) * LEAF, :].astype(F32)
@@ -308,43 +360,7 @@
         return unused
 
     lax.fori_loop(0, PANEL // 256, build, 0)
-    r128 = lax.broadcasted_iota(jnp.int32, (LEAF, LEAF), 0)
-    c128 = lax.broadcasted_iota(jnp.int32, (LEAF, LEAF), 1)
-
-    def step(k, unused):
-        own = pl.ds(pl.multiple_of(k * LEAF, LEAF), LEAF)
-        leaf_factor(a[own, own], leaf)
-        w = jnp.where(r128 >= c128, leaf[...], 0.0)
-        wt = w.T
-        wh, wl = halves(w)
-        th, tl = halves(wt)
-        w3 = jnp.concatenate([wh, wh, wl], axis=1)
-        t3 = jnp.concatenate([th, tl, th], axis=0)
-        ch, cl = halves(a[:, own])
-        lcol = dot(jnp.concatenate([ch, ch, cl], axis=1), t3)
-        a[:, own] = lcol
-        a[own, own] = wt
-        lh, ll = halves(lcol)
-        low[:, 0:LEAF] = lh
-        low[:, LEAF : 2 * LEAF] = lh
-        low[:, 2 * LEAF :] = ll
-        low[own, 0:LEAF] = th
-        low[own, LEAF : 2 * LEAF] = th
-        low[own, 2 * LEAF :] = tl
-
-        def update(j, unused):
-            cols = pl.ds(pl.multiple_of(j * LEAF, LEAF), LEAF)
-            rh, rl = halves(a[own, cols])
-            u = dot(w3, jnp.concatenate([rh, rl, rh], axis=0))
-            uh, ul = halves(u)
-            a[own, cols] = jnp.zeros((LEAF, LEAF), F32)
-            a[:, cols] = a[:, cols] - dot(low[...], jnp.concatenate([uh, ul, uh], axis=0))
-            return unused
-
-        lax.fori_loop(k + 1, count, update, 0)
-        return unused
-
-    lax.fori_loop(0, count, step, 0)
+    chain_steps(a, leaf, low, up)
 
     def finish(k, unused):
         own = pl.ds(pl.multiple_of(k * LEAF, LEAF), LEAF)
@@ -373,6 +389,7 @@
             pltpu.VMEM((PANEL, PANEL), F32),
             pltpu.VMEM((LEAF, LEAF), F32),
             pltpu.VMEM((PANEL, 3 * LEAF), BF16),
+            pltpu.VMEM((3 * LEAF, PANEL), BF16),
             pltpu.VMEM((PANEL, 128), F32),
         ],
         compiler_params=pltpu.CompilerParams(vmem_limit_bytes=60 << 20),
@@ -502,7 +519,8 @@
     pairs = matches.reshape(-1, 128, 2).transpose(0, 2, 1).reshape(-1, 128)
     scaled, panel, panel_extra, extra = gather_panel(embeddings, inverse_scales[None, :], pairs)
     panel = panel.reshape(PANEL, -1)
-    block = lax.all_gather(scaled, "col", axis=0, tiled=True)
+    early = (embeddings.astype(F32) * inverse_scales[None, :]).astype(BF16)
+    block = lax.all_gather(early, "col", axis=0, tiled=True)
     visitors = [
         lax.ppermute(scaled, "row", [((i - s) % row_count, i) for i in range(row_count)])
         for s in range(1, STOPS)

time: 155 us -> 156 us (level); the launches traced: 153 us -> 156 us
  waiting for transfers between devices: 0.05 us -> 17.1 us
  Pallas kernels: 129 us -> 115 us
    all_gather x1, waiting for transfers between devices: 0.02 us -> 17 us  [body(): block = lax.all_gather(early, 'col', axis=0, tiled=True)]
    pallas_call x1, Pallas kernels: 54.1 us -> 41.1 us  [chain(): pl.pallas_call(chain_kernel, out_shape=(jax.ShapeDtypeStruct((PANEL, PANE...]
    unnamed x18 -> x20, local copies, waits for them, and re-layouts: 6.93 us -> 5.82 us
  transfers between devices with their start and end apart: 4 -> 4, of which waited for: 0 -> 1; matrix products, arithmetic and copies ran while one was open for 0% -> 1% of each run, Pallas kernels for 35% -> 26%
where the time goes in v3:
time: 156 us
  Pallas kernels  115 us (74%)
  waiting for transfers between devices  17.1 us (11%)
  between operations  14.1 us (9%)
  local copies, waits for them, and re-layouts  5.82 us (4%)
  starting transfers between devices  2.31 us (1%)
    pallas_call x1, Pallas kernels, gather_panel(): pl.pallas_call(gather_kernel, out_shape=(jax.ShapeDtypeStruct((LEAF, 2048...  43.7 us
    pallas_call x1, Pallas kernels, chain(): pl.pallas_call(chain_kernel, out_shape=(jax.ShapeDtypeStruct((PANEL, PANE...  41.1 us
    pallas_call x1, Pallas kernels, trail(): pl.pallas_call(trail_kernel, out_shape=(jax.ShapeDtypeStruct((1024, STOPS...  30.6 us
    all_gather x1, waiting for transfers between devices, body(): block = lax.all_gather(early, 'col', axis=0, tiled=True)  17 us
    unnamed x20, local copies, waits for them, and re-layouts  5.82 us
  transfers between devices with their start and end apart: 4, of which 1 were waited for; matrix products, arithmetic and copies ran while one was open for 1% of the time, Pallas kernels for 26%

profile of v3, /device:TPU:1, one launch (start us, length us, event | category | flops | bytes accessed | tf_op | source)
XLA Modules:
  0.0 155.5 jit_solution(7212586089890770825)
XLA Ops:
  7.2 0.0 all-gather.2.cloned.1.call-start
  7.2 0.0 copy-start
  7.2 1.0 copy-done
  8.3 0.9 copy-done.1
  9.2 0.0 copy-start.2
  9.2 0.7 copy-done.2
  9.9 43.7 %panel_gather.1 = (bf16[128,2048]{1,0:T(8,128)(2,1)S(1)}, bf16[4,4,2,32,2048]{4,3,2,1,0:T(8,128)(2,1)S(1)}, f32[1,1024]{1,0:T(1,128)S(1)}, f32[1,128]{1,0:T(1,128)S(1)}) custom-call(bf16[128,2048]{1,0:T(8,128)(2,1)S(1)} %copy-done, f32[1,2048]{1,0:T(1,128)S(1)} %bitcast.8, s32[512,128]{1,0:T(8,128)S(1)} %bitcast.7), custom_call_target="tpu_custom_call" | custom-call | tf_op jit(solution)/shard_map/panel_gather/pallas_call | solution.py:262
  53.6 0.0 copy-start.3
  53.6 2.0 %copy-done.3 = bf16[4,4,2,32,2048]{4,3,2,1,0:T(8,128)(2,1)} copy-done((bf16[4,4,2,32,2048]{4,3,2,1,0:T(8,128)(2,1)}, bf16[4,4,2,32,2048]{4,3,2,1,0:T(8,128)(2,1)S(1)}, u32[]{:S(2)}) %copy-start.3) | copy-done | bytes 4194328
  55.5 0.0 copy-start.5
  55.5 0.6 copy-done.5
  56.1 0.0 copy-start.6
  56.1 0.6 copy-done.6
  56.7 0.0 copy-start.4
  56.7 1.7 %collective-permute-start.2 = (bf16[128,2048]{1,0:T(8,128)(2,1)S(1)}, bf16[128,2048]{1,0:T(8,128)(2,1)S(1)}, u32[]{:S(2)}, u32[]{:S(2)}) collective-permute-start(bf16[128,2048]{1,0:T(8,128)(2,1)S(1)} %get-tuple-element.9.own_ref), channel_id=1, source_target_pairs={{232,0},{240,8},{248,16},{0,24},{8,32},{16,40},{24,48},{32,56},{40... | collective-permute-start | bytes 1572872 | tf_op jit(solution)/shard_map/ppermute | solution.py:525
  58.4 0.0 collective-permute-start.1
  58.4 0.6 collective-permute-start
  59.0 0.9 multiply_convert_fusion
  59.9 0.0 all-gather.2.cloned.1.call-update
  59.9 41.1 %panel_chain.1 = (bf16[1024,1024]{1,0:T(8,128)(2,1)}, bf16[1024,1024]{1,0:T(8,128)(2,1)}, f32[1,1024]{1,0:T(1,128)}) custom-call(bf16[1024,2048]{1,0:T(8,128)(2,1)} %bitcast.9, f32[1,1024]{1,0:T(1,128)} %copy-done.5), custom_call_target="tpu_custom_call" | custom-call | flops 99999997952 | bytes 10000000 | tf_op jit(solution)/shard_map/panel_chain/pallas_call | solution.py:379
  101.0 0.0 copy-done.4
  101.0 0.0 collective-permute-done.2.v3_ref
  101.0 0.0 copy-start.7
  101.0 0.0 collective-permute-done.1.v2_ref
  101.0 0.0 copy-start.8
  101.0 0.0 collective-permute-done.v1_ref
  101.1 0.0 copy-start.9
  101.1 17.0 %all-gather.2.cloned.1.call-done.block_ref = bf16[1024,2048]{1,0:T(8,128)(2,1)} async-done(((bf16[128,2048]{1,0:T(8,128)(2,1)}), bf16[1024,2048]{1,0:T(8,128)(2,1)}) %all-gather.2.cloned.1.call-update) | async-done | bytes 4194320 | tf_op jit(solution)/shard_map/all_gather | solution.py:523
  118.1 0.0 copy-done.7
  118.1 0.0 copy-done.8
  118.1 0.0 copy-done.9
  118.1 30.6 %trailing.1 = (f32[1024,512]{1,0:T(8,128)}, f32[128,1024]{1,0:T(8,128)}) custom-call(bf16[1024,2048]{1,0:T(8,128)(2,1)} %all-gather.2.cloned.1.call-done.block_ref, bf16[128,2048]{1,0:T(8,128)(2,1)} %copy-done.4, bf16[128,2048]{1,0:T(8,128)(2,1)} %copy-done.9, bf16[128,2048]{1,0:T(8,128)(2,1)} %copy-done.8, bf16[128,2048]{1,0:T(8,128)(2,1)} %copy-done.7, ...), custom_call_target="tpu_custom_call" | custom-call | flops 30000001024 | bytes 20000000 | tf_op jit(solution)/shard_map/trailing/pallas_call | solution.py:492
  (1 shorter events, 0.0 us)
Async XLA Ops:
  7.2 110.9 %all-gather.2.cloned.1.call-start = ((), (), s32[]{:S(2)}) async-start(), calls=%async_computation | async-start | bytes 4718592 | tf_op jit(solution)/shard_map/all_gather | solution.py:523
  7.2 1.0 copy-start
  8.3 0.9 copy-start.1
  9.2 0.7 copy-start.2
  53.6 2.0 %copy-start.3 = (bf16[4,4,2,32,2048]{4,3,2,1,0:T(8,128)(2,1)}, bf16[4,4,2,32,2048]{4,3,2,1,0:T(8,128)(2,1)S(1)}, u32[]{:S(2)}) copy-start(bf16[4,4,2,32,2048]{4,3,2,1,0:T(8,128)(2,1)S(1)} %get-tuple-element.10) | copy-start | bytes 12582916
  55.5 0.6 copy-start.5
  56.1 0.6 copy-start.6
  56.7 44.3 %copy-start.4 = (bf16[128,2048]{1,0:T(8,128)(2,1)}, bf16[128,2048]{1,0:T(8,128)(2,1)S(1)}, u32[]{:S(2)}) copy-start(bf16[128,2048]{1,0:T(8,128)(2,1)S(1)} %get-tuple-element.9.own_ref) | copy-start | bytes 1572868
  56.7 44.3 %collective-permute-start.2 = (bf16[128,2048]{1,0:T(8,128)(2,1)S(1)}, bf16[128,2048]{1,0:T(8,128)(2,1)S(1)}, u32[]{:S(2)}, u32[]{:S(2)}) collective-permute-start(bf16[128,2048]{1,0:T(8,128)(2,1)S(1)} %get-tuple-element.9.own_ref), channel_id=1, source_target_pairs={{232,0},{240,8},{248,16},{0,24},{8,32},{16,40},{24,48},{32,56},{40... | collective-permute-start | bytes 1572872 | tf_op jit(solution)/shard_map/ppermute | solution.py:525
  58.4 42.7 %collective-permute-start.1 = (bf16[128,2048]{1,0:T(8,128)(2,1)S(1)}, bf16[128,2048]{1,0:T(8,128)(2,1)S(1)}, u32[]{:S(2)}, u32[]{:S(2)}) collective-permute-start(bf16[128,2048]{1,0:T(8,128)(2,1)S(1)} %get-tuple-element.9.own_ref), channel_id=1, source_target_pairs={{240,0},{248,8},{0,16},{8,24},{16,32},{24,40},{32,48},{40,56},{48,... | collective-permute-start | bytes 1572872 | tf_op jit(solution)/shard_map/ppermute | solution.py:525
  58.4 42.7 %collective-permute-start = (bf16[128,2048]{1,0:T(8,128)(2,1)S(1)}, bf16[128,2048]{1,0:T(8,128)(2,1)S(1)}, u32[]{:S(2)}, u32[]{:S(2)}) collective-permute-start(bf16[128,2048]{1,0:T(8,128)(2,1)S(1)} %get-tuple-element.9.own_ref), channel_id=1, source_target_pairs={{248,0},{0,8},{8,16},{16,24},{24,32},{32,40},{40,48},{48,56},{56,6... | collective-permute-start | bytes 1572872 | tf_op jit(solution)/shard_map/ppermute | solution.py:525
  101.0 17.1 %copy-start.7 = (bf16[128,2048]{1,0:T(8,128)(2,1)}, bf16[128,2048]{1,0:T(8,128)(2,1)S(1)}, u32[]{:S(2)}) copy-start(bf16[128,2048]{1,0:T(8,128)(2,1)S(1)} %collective-permute-done.2.v3_ref) | copy-start | bytes 1572868
  101.0 17.1 %copy-start.8 = (bf16[128,2048]{1,0:T(8,128)(2,1)}, bf16[128,2048]{1,0:T(8,128)(2,1)S(1)}, u32[]{:S(2)}) copy-start(bf16[128,2048]{1,0:T(8,128)(2,1)S(1)} %collective-permute-done.1.v2_ref) | copy-start | bytes 1572868
  101.1 17.1 %copy-start.9 = (bf16[128,2048]{1,0:T(8,128)(2,1)}, bf16[128,2048]{1,0:T(8,128)(2,1)S(1)}, u32[]{:S(2)}) copy-start(bf16[128,2048]{1,0:T(8,128)(2,1)S(1)} %collective-permute-done.v1_ref) | copy-start | bytes 1572868
Sparse Core Ops, SparseCore 0:
  60.0 58.0 all-gather.1

commit v4 on v2

v4 whole, which is shorter than its diff:
```python
import functools

import jax
import jax.numpy as jnp
from jax import lax
from jax.experimental import pallas as pl
from jax.experimental.pallas import tpu as pltpu
from jax.sharding import PartitionSpec as P

PANEL = 1024
STOPS = 4
LEAF = 128
AHEAD = 4
RING_THREE = 1
RING_FOUR = 5
F32 = jnp.float32
BF16 = jnp.bfloat16


def halves(x):
    high = x.astype(BF16)
    return high, (x - high.astype(F32)).astype(BF16)


def dot(a, b):
    return jnp.dot(a, b, preferred_element_type=F32)


def dot_nt(a, b):
    return lax.dot_general(a, b, (((1,), (1,)), ((), ())), preferred_element_type=F32)


def leaf_factor(tile, out_ref):
    n = LEAF
    groups = n // 8
    lane = lax.broadcasted_iota(jnp.int32, (8, 128), 1)
    rows = [tile[8 * i : 8 * i + 8, :] for i in range(groups)]

    def column(i, k):
        return jnp.broadcast_to(rows[i][:, k : k + 1], (8, 128))

    def one_row(x, r):
        return jnp.broadcast_to(x[r : r + 1, :], (8, 128))

    pending = [[column(i, k) for i in range(groups)] for k in range(AHEAD)]
    for k in range(n):
        g, r = divmod(k, 8)
        current = pending.pop(0)
        scale = lax.rsqrt(one_row(current[g], r))
        c = [current[i] * scale if i >= g else None for i in range(groups)]
        if k + AHEAD < n:
            pending.append([column(i, k + AHEAD) if i >= (k + AHEAD) // 8 else None for i in range(groups)])
        for j in range(len(pending)):
            gp, rp = divmod(k + 1 + j, 8)
            s = one_row(c[gp], rp)
            pending[j] = [pending[j][i] - c[i] * s if i >= gp else None for i in range(groups)]
        u = jnp.where(lane == k, scale, one_row(rows[g], r) * scale)
        out_ref[k : k + 1, :] = u[0:1, :]
        for i in range(g, groups):
            rows[i] = jnp.where(lane == k, 0.0, rows[i]) - c[i] * u


MESH = pl.DeviceIdType.MESH
SIDE = 4


def counts_step(values, first):
    sub32 = lax.broadcasted_iota(jnp.int32, (32, 128), 0)
    sub16 = lax.broadcasted_iota(jnp.int32, (16, 128), 0)
    place = jnp.where((values & 1023) < 32, values & 31, -1)
    inside = values - first
    part = jnp.where((inside >= 0) & (inside < 128), inside >> 4, -1)
    left = jnp.concatenate(
        [jnp.where(sub32 == values >> 10, 1.0, 0.0), jnp.where(sub16 == part, 1.0, 0.0)], axis=0
    ).astype(BF16)
    right = jnp.concatenate(
        [jnp.where(sub32 == place, 1.0, 0.0), jnp.where(sub16 == (values & 15), 1.0, 0.0)], axis=0
    ).astype(BF16)
    return left, right


def spread(table, width):
    n = table.shape[0]
    total = n * width
    tiled = jnp.concatenate([table] * n, axis=1)
    row = lax.broadcasted_iota(jnp.int32, (n, total), 0)
    lane = lax.broadcasted_iota(jnp.int32, (n, total), 1)
    return jnp.sum(jnp.where(lane >> (width.bit_length() - 1) == row, tiled, 0.0), axis=0, keepdims=True)


def to_lanes(column):
    return jnp.broadcast_to(column, (128, 128)).T[0:1, :]


def chain_steps(a, leaf, low, up, event):
    count = PANEL // LEAF
    r128 = lax.broadcasted_iota(jnp.int32, (LEAF, LEAF), 0)
    c128 = lax.broadcasted_iota(jnp.int32, (LEAF, LEAF), 1)
    lane = lax.broadcasted_iota(jnp.int32, (LEAF, PANEL), 1)

    def beside(x):
        high, lo = halves(x)
        return jnp.concatenate([high, high, lo], axis=1)

    def above(x):
        high, lo = halves(x)
        return jnp.concatenate([high, lo, high], axis=0)

    def inverse():
        w = jnp.where(r128 >= c128, leaf[...], 0.0)
        return w, w.T

    def block(k):
        return pl.ds(pl.multiple_of(k * LEAF, LEAF), LEAF)

    leaf_factor(a[0:LEAF, 0:LEAF], leaf)

    def step(m, unused):
        event(m)
        own, after = block(m), block(m + 1)
        w, wt = inverse()
        w3, t3 = beside(w), above(wt)
        next_low = dot(beside(a[after, own]), t3)
        next_up = dot(w3, above(a[own, after]))
        tile = a[after, after] - dot(beside(next_low), above(next_up))
        lcol = dot(beside(a[:, own]), t3)
        a[:, own] = lcol
        a[own, own] = wt
        low[...] = beside(lcol)
        low[own, :] = beside(wt)
        mine = a[own, :]
        later = lane >= (m + 1) * LEAF
        up[...] = above(jnp.where(later, dot(w3, above(mine)), 0.0))
        a[own, :] = jnp.where(later, 0.0, mine)
        for n in range(PANEL // 256):
            cols = slice(256 * n, 256 * n + 256)
            a[:, cols] = a[:, cols] - dot(low[...], up[:, cols])
        leaf_factor(tile, leaf)
        return unused

    lax.fori_loop(0, count - 1, step, 0)
    last = block(count - 1)
    w, wt = inverse()
    a[:, last] = dot(beside(a[:, last]), above(wt))
    a[last, last] = wt


def whole_kernel(
    emb_ref, inv_ref, pairs_ref, trail_ref, factor_ref,
    rows, panel, pextra, extra, hits, a, leaf, low, up, psq_col, psq_row, sq_col, sq_row,
    kh, kl, xh, xl, fh, fl, vh, vl, zs, zr, ss, sr, cs, cr, bs, br, vs, vr,
):
    me = lax.axis_index("row")
    slot = lax.axis_index("col")
    x, y, core = me // 8, (me // 2) % SIDE, me % 2
    xp, xm, xo = (x + 1) % SIDE, (x + 3) % SIDE, (x + 2) % SIDE
    yp, ym, yo = (y + 1) % SIDE, (y + 3) % SIDE, (y + 2) % SIDE

    def row_at(x, y, core):
        return (x * SIDE + y) * 2 + core

    to_xp, to_xm = row_at(xp, y, core), row_at(xm, y, core)
    to_yp, to_ym = row_at(x, yp, core), row_at(x, ym, core)
    twin = row_at(x, y, 1 - core)
    barrier = pltpu.get_barrier_semaphore()
    for other in (to_xp, to_xm, to_yp, to_ym, twin):
        pl.semaphore_signal(barrier, inc=1, device_id=(other, slot), device_id_type=MESH)
    for j in range(1, 8):
        pl.semaphore_signal(barrier, inc=1, device_id=(me, (slot + j) % 8), device_id_type=MESH)
    for j in range(1, STOPS):
        pl.semaphore_signal(barrier, inc=1, device_id=((me + j) % 32, slot), device_id_type=MESH)
        pl.semaphore_signal(barrier, inc=1, device_id=((me + 32 - j) % 32, slot), device_id_type=MESH)

    def scale(start, count):
        v = emb_ref[start : start + count, :].astype(F32) * inv_ref[0:1, :]
        rows[slot, start : start + count, :] = v.astype(BF16)

    scale(0, 32)

    @pl.when(slot == 0)
    def _():
        panel[x, y, core] = rows[slot, 0:32, :]

    pl.semaphore_wait(barrier, 12 + 2 * (STOPS - 1))

    def copy(view, row, col, send, recv):
        return pltpu.make_async_remote_copy(
            src_ref=view, dst_ref=view, send_sem=send, recv_sem=recv, device_id=(row, col), device_id_type=MESH
        )

    def chunk(q):
        return panel.at[x, y, core, :, pl.ds(pl.multiple_of(q * 256, 256), 256)]

    @pl.when(slot == 0)
    def _():
        for c in range(1, 8):
            copy(chunk(c), me, c, zs.at[c], zr.at[c]).start()
        for c in range(1, 8):
            copy(chunk(0), me, c, zs.at[7 + c], zr.at[0]).start()

    scale(32, 96)

    @pl.when(slot != 0)
    def _():
        copy(chunk(slot), me, slot, zs.at[0], zr.at[slot]).wait_recv()
        for j in range(1, 8):
            other = (slot + j) % 8

            @pl.when(other != 0)
            def _(other=other, j=j):
                copy(chunk(slot), me, other, zs.at[j], zr.at[slot]).start()

    first = row_at(x, y, core) * 1024 + slot * 128

    def count(i, total):
        lefts, rights = [], []
        for r in range(8):
            left, right = counts_step(jnp.broadcast_to(pairs_ref[pl.ds(i * 8 + r, 1), :], (8, 128))[0:1, :], first)
            lefts.append(left)
            rights.append(right)
        return total + dot_nt(jnp.concatenate(lefts, axis=1), jnp.concatenate(rights, axis=1))

    hits[:, 0:48] = lax.fori_loop(0, pairs_ref.shape[0] // 8, count, jnp.zeros((48, 48), F32))

    @pl.when(slot != 0)
    def _():
        for j in range(1, 8):
            other = (slot + j) % 8
            copy(chunk(other), me, slot, zs.at[0], zr.at[other]).wait_recv()

    upper, lower = pl.ds(0, 64), pl.ds(64, 64)

    def ring_views(h):
        up, down = (slot + 9 - h) % 8, (slot + 7 + h) % 8
        if h < 4:
            return rows.at[up], rows.at[down]
        return rows.at[up, upper], rows.at[down, lower]

    def arriving_views(h):
        up, down = (slot + 8 - h) % 8, (slot + h) % 8
        if h < 4:
            return rows.at[up], rows.at[down]
        return rows.at[up, upper], rows.at[down, lower]

    def ring_send(h):
        up, down = ring_views(h)
        copy(up, me, (slot + 1) % 8, bs.at[2 * h - 2], br.at[2 * h - 2]).start()
        copy(down, me, (slot + 7) % 8, bs.at[2 * h - 1], br.at[2 * h - 1]).start()

    def ring_arrive(h):
        up, down = arriving_views(h)
        copy(up, me, slot, bs.at[2 * h - 2], br.at[2 * h - 2]).wait_recv()
        copy(down, me, slot, bs.at[2 * h - 1], br.at[2 * h - 1]).wait_recv()

    def ring_sent(h):
        up, down = ring_views(h)
        copy(up, me, slot, bs.at[2 * h - 2], br.at[2 * h - 2]).wait_send()
        copy(down, me, slot, bs.at[2 * h - 1], br.at[2 * h - 1]).wait_send()

    def visit(j):
        return pltpu.make_async_remote_copy(
            src_ref=rows.at[slot], dst_ref=rows.at[7 + j], send_sem=vs.at[j - 1], recv_sem=vr.at[j - 1],
            device_id=((me + j) % 32, slot), device_id_type=MESH,
        )

    ring_send(1)
    near, far = pl.ds(0, 1024), pl.ds(1024, 1024)
    sent = []

    def send(view, row, i):
        c = copy(view, row, slot, ss.at[i], sr.at[i])
        c.start()
        sent.append(c)

    def arrive(view, i):
        copy(view, twin, slot, ss.at[i], sr.at[i]).wait_recv()

    passed = []

    def share(view, back, i):
        c = copy(view, twin, slot, cs.at[i], cr.at[i])
        c.start()
        passed.append((c, back, i))

    own_near, own_far = panel.at[x, y, core, :, near], panel.at[x, y, core, :, far]
    send(own_near, to_xp, 0)
    send(own_far, to_yp, 1)
    send(own_near, to_xm, 2)
    send(own_far, to_ym, 3)
    share(panel.at[x, y, core], panel.at[x, y, 1 - core], 0)
    top, bottom = pl.ds(0, 16), pl.ds(16, 16)
    arrive(panel.at[xm, y, core, :, near], 0)
    send(panel.at[xm, y, core, top, near], to_xp, 4)
    arrive(panel.at[x, ym, core, :, far], 1)
    send(panel.at[x, ym, core, top, far], to_yp, 5)
    arrive(panel.at[xp, y, core, :, near], 2)
    send(panel.at[xp, y, core, bottom, near], to_xm, 6)
    arrive(panel.at[x, yp, core, :, far], 3)
    send(panel.at[x, yp, core, bottom, far], to_ym, 7)
    share(panel.at[xm, y, core, :, near], panel.at[xm, y, 1 - core, :, near], 1)
    share(panel.at[x, ym, core, :, far], panel.at[x, ym, 1 - core, :, far], 2)
    share(panel.at[xp, y, core, :, near], panel.at[xp, y, 1 - core, :, near], 3)
    share(panel.at[x, yp, core, :, far], panel.at[x, yp, 1 - core, :, far], 4)
    arrive(panel.at[xo, y, core, top, near], 4)
    arrive(panel.at[xo, y, core, bottom, near], 6)
    send(panel.at[:, y, core, :, near], to_yp, 8)
    send(panel.at[:, y, core, :, near], to_ym, 10)
    arrive(panel.at[x, yo, core, top, far], 5)
    arrive(panel.at[x, yo, core, bottom, far], 7)
    send(panel.at[x, :, core, :, far], to_xp, 9)
    send(panel.at[x, :, core, :, far], to_xm, 11)
    share(panel.at[xo, y, core, :, near], panel.at[xo, y, 1 - core, :, near], 5)
    share(panel.at[x, yo, core, :, far], panel.at[x, yo, 1 - core, :, far], 6)

    ring_arrive(1)
    ring_send(2)
    row_hits = hits[:, 0:48]
    pextra[...] = 0.1 + 0.5 * spread(row_hits[0:32, 0:32], 32)
    extra[...] = 0.1 + 0.5 * spread(row_hits[32:40, 32:48], 16)

    first_two, last_two = pl.ds(0, 2), pl.ds(2, 2)
    arrive(panel.at[:, ym, core, :, near], 8)
    send(panel.at[first_two, ym, core, :, near], to_yp, 12)
    arrive(panel.at[xm, :, core, :, far], 9)
    send(panel.at[xm, first_two, core, :, far], to_xp, 13)
    arrive(panel.at[:, yp, core, :, near], 10)
    send(panel.at[last_two, yp, core, :, near], to_ym, 14)
    arrive(panel.at[xp, :, core, :, far], 11)
    send(panel.at[xp, last_two, core, :, far], to_xm, 15)
    share(panel.at[:, ym, core, :, near], panel.at[:, ym, 1 - core, :, near], 7)
    share(panel.at[xm, :, core, :, far], panel.at[xm, :, 1 - core, :, far], 8)
    share(panel.at[:, yp, core, :, near], panel.at[:, yp, 1 - core, :, near], 9)
    share(panel.at[xp, :, core, :, far], panel.at[xp, :, 1 - core, :, far], 10)
    arrive(panel.at[first_two, yo, core, :, near], 12)
    arrive(panel.at[last_two, yo, core, :, near], 14)
    share(panel.at[:, yo, core, :, near], panel.at[:, yo, 1 - core, :, near], 11)
    arrive(panel.at[xo, first_two, core, :, far], 13)
    arrive(panel.at[xo, last_two, core, :, far], 15)
    share(panel.at[xo, :, core, :, far], panel.at[xo, :, 1 - core, :, far], 12)
    for c, back, i in passed:
        copy(back, twin, slot, cs.at[i], cr.at[i]).wait_recv()
        c.wait_send()
    for j in range(1, STOPS):
        visit(j).start()

    def panel_rows(n):
        return panel[n].reshape(256, 2048)

    def panel_squares(n, unused):
        for q in range(2):
            v = panel_rows(n)[q * LEAF : (q + 1) * LEAF, :].astype(F32)
            s = jnp.sum(v * v, axis=1, keepdims=True)
            at = pl.ds(pl.multiple_of(n * 256 + q * LEAF, LEAF), LEAF)
            psq_col[at, :] = jnp.broadcast_to(s, (LEAF, 128))
            psq_row[0:1, at] = to_lanes(s)
        return unused

    lax.fori_loop(0, SIDE, panel_squares, 0)

    def build(n, unused):
        cols = pl.ds(pl.multiple_of(n * 256, 256), 256)
        g = dot_nt(panel[...].reshape(PANEL, 2048), panel_rows(n))
        s = psq_col[...]
        k = jnp.exp(-0.5 * (jnp.concatenate([s, s], axis=1) + psq_row[0:1, cols] - 2.0 * g))
        row = lax.broadcasted_iota(jnp.int32, (PANEL, 256), 0)
        lane = lax.broadcasted_iota(jnp.int32, (PANEL, 256), 1)
        a[:, cols] = k + jnp.where(row == lane + n * 256, pextra[0:1, cols], 0.0)
        return unused

    lax.fori_loop(0, SIDE, build, 0)

    def event(m):
        @pl.when(m == RING_THREE)
        def _():
            ring_arrive(2)
            ring_send(3)

        @pl.when(m == RING_FOUR)
        def _():
            ring_arrive(3)
            ring_send(4)

    chain_steps(a, leaf, low, up, event)

    def finish(k, unused):
        own = pl.ds(pl.multiple_of(k * LEAF, LEAF), LEAF)
        row = lax.broadcasted_iota(jnp.int32, (PANEL, LEAF), 0)
        value = jnp.where(row < (k + 1) * LEAF, a[:, own], 0.0)
        high, lo = halves(value)
        xh[:, own] = high
        xl[:, own] = lo
        return unused

    lax.fori_loop(0, PANEL // LEAF, finish, 0)
    ring_arrive(4)
    for j in range(1, STOPS):
        visit(j).wait_recv()
    total = 1024 + 3 * LEAF

    def all_rows():
        return rows[...].reshape(total, 2048)

    def squares(i, unused):
        v = rows[i].astype(F32)
        s = jnp.sum(v * v, axis=1, keepdims=True)
        sq_col[pl.ds(pl.multiple_of(i * LEAF, LEAF), LEAF), :] = jnp.broadcast_to(s, (LEAF, 128))
        return unused

    lax.fori_loop(0, total // LEAF, squares, 0)
    own = pl.ds(pl.multiple_of(slot * LEAF, LEAF), LEAF)
    sq_row[0:1, 0:128] = sq_col[own, :].T[0:1, :]
    for s in range(3):
        sq_row[0:1, (s + 1) * LEAF : (s + 2) * LEAF] = sq_col[1024 + s * LEAF : 1024 + (s + 1) * LEAF, :].T[0:1, :]
    lead_row = lax.broadcasted_iota(jnp.int32, (32, 256), 0)
    lead_lane = lax.broadcasted_iota(jnp.int32, (32, 256), 1)

    def kernel_part(n, unused):
        cols = pl.ds(pl.multiple_of(n * 256, 256), 256)
        g = dot_nt(all_rows(), panel_rows(n))
        s = sq_col[...]
        k = jnp.exp(-0.5 * (jnp.concatenate([s, s], axis=1) + psq_row[0:1, cols] - 2.0 * g))
        high, lo = halves(k)
        kh[:, cols] = high
        kl[:, cols] = lo
        more = pextra[0:1, cols]

        def fix(start, block, scale):
            part = k[start : start + 32, :]
            hit = lead_lane + n * 256 == block * 32 + lead_row
            part = part + jnp.where(hit, more * scale, 0.0)
            high, lo = halves(part)
            kh[start : start + 32, cols] = high
            kl[start : start + 32, cols] = lo

        fix(0, me, 1.0)
        lead = jnp.where(slot == 0, 1.0, 0.0).astype(F32)
        for s in range(3):
            fix(1024 + s * LEAF, (me + 31 - s) % 32, lead)
        return unused

    lax.fori_loop(0, SIDE, kernel_part, 0)
    for n in range(4):
        depth = 256 * (n + 1)
        cols = slice(256 * n, 256 * n + 256)
        f = dot(kh[:, :depth], xh[:depth, cols])
        f = f + dot(kh[:, :depth], xl[:depth, cols])
        f = f + dot(kl[:, :depth], xh[:depth, cols])
        high, lo = halves(f)
        fh[:, cols] = high
        fl[:, cols] = lo
    factor_ref[...] = fh[own, :].astype(F32) + fl[own, :].astype(F32)
    vh[0:LEAF, :] = fh[own, :]
    vl[0:LEAF, :] = fl[own, :]
    vh[LEAF:, :] = fh[1024:, :]
    vl[LEAF:, :] = fl[1024:, :]
    r = lax.broadcasted_iota(jnp.int32, (256, LEAF), 0)
    c = lax.broadcasted_iota(jnp.int32, (256, LEAF), 1)

    def tile(i, unused):
        at = pl.ds(pl.multiple_of(i * 256, 256), 256)
        left = rows[pl.ds(2 * i, 2)].reshape(256, 2048)
        g = jnp.concatenate([dot_nt(left, rows[slot]), dot_nt(left, rows[8:11].reshape(3 * LEAF, 2048))], axis=1)
        s = sq_col[at, :]
        k = jnp.exp(-0.5 * (jnp.concatenate([s] * 4, axis=1) + sq_row[...] - 2.0 * g))
        ff = dot_nt(fh[at, :], vh[...])
        ff = ff + dot_nt(fh[at, :], vl[...])
        ff = ff + dot_nt(fl[at, :], vh[...])
        t = k - ff
        trail_ref[at, :] = t
        diagonal = jnp.where(r + i * 256 == c + slot * LEAF, extra[0:1, :], 0.0)
        trail_ref[at, 0:LEAF] = t[:, 0:LEAF] + diagonal
        return unused

    lax.fori_loop(0, 4, tile, 0)
    for h in range(1, 5):
        ring_sent(h)
    for j in range(1, STOPS):
        visit(j).wait_send()
    for c in sent:
        c.wait_send()

    @pl.when(slot == 0)
    def _():
        for c in range(1, 8):
            copy(chunk(c), me, c, zs.at[c], zr.at[c]).wait_send()
            copy(chunk(0), me, c, zs.at[7 + c], zr.at[0]).wait_send()

    @pl.when(slot != 0)
    def _():
        for j in range(1, 8):
            other = (slot + j) % 8

            @pl.when(other != 0)
            def _(other=other, j=j):
                copy(chunk(slot), me, other, zs.at[j], zr.at[slot]).wait_send()


def whole(embeddings, inverse_scales, pairs):
    vmem = pl.BlockSpec(memory_space=pltpu.VMEM)
    total = 1024 + 3 * LEAF
    return pl.pallas_call(
        whole_kernel,
        out_shape=(
            jax.ShapeDtypeStruct((1024, STOPS * LEAF), F32),
            jax.ShapeDtypeStruct((LEAF, PANEL), F32),
        ),
        in_specs=[vmem] * 3,
        out_specs=(vmem, vmem),
        scratch_shapes=[
            pltpu.VMEM((11, LEAF, 2048), BF16),
            pltpu.VMEM((SIDE, SIDE, 2, 32, 2048), BF16),
            pltpu.VMEM((1, PANEL), F32),
            pltpu.VMEM((1, LEAF), F32),
            pltpu.VMEM((48, 128), F32),
            pltpu.VMEM((PANEL, PANEL), F32),
            pltpu.VMEM((LEAF, LEAF), F32),
            pltpu.VMEM((PANEL, 3 * LEAF), BF16),
            pltpu.VMEM((3 * LEAF, PANEL), BF16),
            pltpu.VMEM((PANEL, 128), F32),
            pltpu.VMEM((1, PANEL), F32),
            pltpu.VMEM((total, 128), F32),
            pltpu.VMEM((1, STOPS * LEAF), F32),
            pltpu.VMEM((total, PANEL), BF16),
            pltpu.VMEM((total, PANEL), BF16),
            pltpu.VMEM((PANEL, PANEL), BF16),
            pltpu.VMEM((PANEL, PANEL), BF16),
            pltpu.VMEM((total, PANEL), BF16),
            pltpu.VMEM((total, PANEL), BF16),
            pltpu.VMEM((STOPS * LEAF, PANEL), BF16),
            pltpu.VMEM((STOPS * LEAF, PANEL), BF16),
            pltpu.SemaphoreType.DMA((15,)),
            pltpu.SemaphoreType.DMA((8,)),
            pltpu.SemaphoreType.DMA((16,)),
            pltpu.SemaphoreType.DMA((16,)),
            pltpu.SemaphoreType.DMA((13,)),
            pltpu.SemaphoreType.DMA((13,)),
            pltpu.SemaphoreType.DMA((8,)),
            pltpu.SemaphoreType.DMA((8,)),
            pltpu.SemaphoreType.DMA((3,)),
            pltpu.SemaphoreType.DMA((3,)),
        ],
        compiler_params=pltpu.CompilerParams(
            collective_id=0, has_side_effects=True, vmem_limit_bytes=60 << 20
        ),
        name="whole",
    )(embeddings, inverse_scales, pairs)


def body(embeddings, inverse_scales, matches):
    pairs = matches.reshape(-1, 128, 2).transpose(0, 2, 1).reshape(-1, 128)
    return whole(embeddings, inverse_scales[None, :], pairs)


def solution(mesh):
    return jax.shard_map(
        body,
        mesh=mesh,
        in_specs=(P(("row", "col"), None), P(), P()),
        out_specs=(P("row", "col"), P(("row", "col"), None)),
        check_vma=False,
    )
```

time: 155 us -> 115 us (0.74); the launches traced: 153 us -> 114 us
  Pallas kernels: 129 us -> 110 us
  between operations: 14.1 us -> 0.65 us
  local copies, waits for them, and re-layouts: 6.93 us -> 3.93 us
  starting transfers between devices: 2.39 us -> 0 us
    pallas_call x3 -> x1, Pallas kernels: 129 us -> 110 us  [whole(): pl.pallas_call(whole_kernel, out_shape=(jax.ShapeDtypeStruct((1024, STOPS...]
    unnamed x18 -> x4, local copies, waits for them, and re-layouts: 6.93 us -> 3.93 us
    ppermute x3 -> x0, starting transfers between devices: 2.35 us -> none  [body(): lax.ppermute(scaled, 'row', [((i - s) % row_count, i) for i in range(row_...]
  transfers between devices with their start and end apart: 4 -> 0, of which waited for: 0 -> 0; matrix products, arithmetic and copies ran while one was open for 0% -> 0% of each run, Pallas kernels for 35% -> 0%
where the time goes in v4:
time: 115 us; the launch traced here: 114 us
  Pallas kernels  110 us (96%)
  local copies, waits for them, and re-layouts  3.93 us (3%)
    pallas_call x1, Pallas kernels, whole(): pl.pallas_call(whole_kernel, out_shape=(jax.ShapeDtypeStruct((1024, STOPS...  110 us
    unnamed x4, local copies, waits for them, and re-layouts  3.93 us

profile of v4, /device:TPU:1, one launch (start us, length us, event | category | flops | bytes accessed | tf_op | source)
XLA Modules:
  0.0 114.5 jit_solution(9277550160523171630)
XLA Ops:
  0.6 109.9 %whole.1 = (f32[1024,512]{1,0:T(8,128)}, f32[128,1024]{1,0:T(8,128)}) custom-call(bf16[128,2048]{1,0:T(8,128)(2,1)} %emb_ref.1, f32[1,2048]{1,0:T(1,128)} %bitcast.7, s32[512,128]{1,0:T(8,128)} %bitcast.6), custom_call_target="tpu_custom_call" | custom-call | tf_op jit(solution)/shard_map/whole/pallas_call | solution.py:501
  110.6 0.0 copy-start
  110.6 3.1 %copy.8 = f32[1024,512]{1,0:T(8,128)} copy(f32[1024,512]{1,0:T(8,128)} %get-tuple-element.4) | data formatting | bytes 4194304
  113.7 0.0 copy-done
  113.7 0.8 copy.9
Async XLA Ops:
  110.6 3.1 %copy-start = (f32[128,1024]{1,0:T(8,128)S(1)}, f32[128,1024]{1,0:T(8,128)}, u32[]{:S(2)}) copy-start(f32[128,1024]{1,0:T(8,128)} %get-tuple-element.5) | copy-start | bytes 1572868

commit v5 on v4

--- a/solution.py
+++ b/solution.py
@@ -11,8 +11,6 @@
 STOPS = 4
 LEAF = 128
 AHEAD = 4
-RING_THREE = 1
-RING_FOUR = 5
 F32 = jnp.float32
 BF16 = jnp.bfloat16
 
@@ -67,16 +65,22 @@
 def counts_step(values, first):
     sub32 = lax.broadcasted_iota(jnp.int32, (32, 128), 0)
     sub16 = lax.broadcasted_iota(jnp.int32, (16, 128), 0)
+    block = values >> 10
     place = jnp.where((values & 1023) < 32, values & 31, -1)
     inside = values - first
     part = jnp.where((inside >= 0) & (inside < 128), inside >> 4, -1)
-    left = jnp.concatenate(
-        [jnp.where(sub32 == values >> 10, 1.0, 0.0), jnp.where(sub16 == part, 1.0, 0.0)], axis=0
-    ).astype(BF16)
-    right = jnp.concatenate(
-        [jnp.where(sub32 == place, 1.0, 0.0), jnp.where(sub16 == (values & 15), 1.0, 0.0)], axis=0
-    ).astype(BF16)
-    return left, right
+    unit = values & 15
+
+    def marks(big, small, r):
+        return jnp.concatenate(
+            [
+                jnp.where(sub32 == big[r : r + 1, :], 1.0, 0.0).astype(BF16),
+                jnp.where(sub16 == small[r : r + 1, :], 1.0, 0.0).astype(BF16),
+            ],
+            axis=0,
+        )
+
+    return [marks(block, part, r) for r in range(8)], [marks(place, unit, r) for r in range(8)]
 
 
 def spread(table, width):
@@ -92,7 +96,7 @@
     return jnp.broadcast_to(column, (128, 128)).T[0:1, :]
 
 
-def chain_steps(a, leaf, low, up, event):
+def chain_steps(a, leaf, low, up, xh, xl, event, one_slice, two_slices):
     count = PANEL // LEAF
     r128 = lax.broadcasted_iota(jnp.int32, (LEAF, LEAF), 0)
     c128 = lax.broadcasted_iota(jnp.int32, (LEAF, LEAF), 1)
@@ -113,9 +117,16 @@
     def block(k):
         return pl.ds(pl.multiple_of(k * LEAF, LEAF), LEAF)
 
+    def finish_column(m, lcol, wt):
+        low[...] = beside(lcol)
+        low[block(m), :] = beside(wt)
+        row = lax.broadcasted_iota(jnp.int32, (PANEL, LEAF), 0)
+        for half, out in ((slice(0, LEAF), xh), (slice(2 * LEAF, 3 * LEAF), xl)):
+            out[:, block(m)] = jnp.where(row < (m + 1) * LEAF, low[:, half].astype(F32), 0.0).astype(BF16)
+
     leaf_factor(a[0:LEAF, 0:LEAF], leaf)
 
-    def step(m, unused):
+    def step(beside_leaf, m, unused):
         event(m)
         own, after = block(m), block(m + 1)
         w, wt = inverse()
@@ -123,11 +134,7 @@
         next_low = dot(beside(a[after, own]), t3)
         next_up = dot(w3, above(a[own, after]))
         tile = a[after, after] - dot(beside(next_low), above(next_up))
-        lcol = dot(beside(a[:, own]), t3)
-        a[:, own] = lcol
-        a[own, own] = wt
-        low[...] = beside(lcol)
-        low[own, :] = beside(wt)
+        finish_column(m, dot(beside(a[:, own]), t3), wt)
         mine = a[own, :]
         later = lane >= (m + 1) * LEAF
         up[...] = above(jnp.where(later, dot(w3, above(mine)), 0.0))
@@ -135,14 +142,15 @@
         for n in range(PANEL // 256):
             cols = slice(256 * n, 256 * n + 256)
             a[:, cols] = a[:, cols] - dot(low[...], up[:, cols])
+        beside_leaf(m)
         leaf_factor(tile, leaf)
         return unused
 
-    lax.fori_loop(0, count - 1, step, 0)
+    lax.fori_loop(0, 3, functools.partial(step, one_slice), 0)
+    lax.fori_loop(3, count - 1, functools.partial(step, two_slices), 0)
     last = block(count - 1)
     w, wt = inverse()
-    a[:, last] = dot(beside(a[:, last]), above(wt))
-    a[last, last] = wt
+    finish_column(count - 1, dot(beside(a[:, last]), above(wt)), wt)
 
 
 def whole_kernel(
@@ -163,7 +171,7 @@
     to_yp, to_ym = row_at(x, yp, core), row_at(x, ym, core)
     twin = row_at(x, y, 1 - core)
     barrier = pltpu.get_barrier_semaphore()
-    for other in (to_xp, to_xm, to_yp, to_ym, twin):
+    for other in (to_xp, to_xm, to_yp, to_ym, twin, row_at(xo, y, core), row_at(x, yo, core)):
         pl.semaphore_signal(barrier, inc=1, device_id=(other, slot), device_id_type=MESH)
     for j in range(1, 8):
         pl.semaphore_signal(barrier, inc=1, device_id=(me, (slot + j) % 8), device_id_type=MESH)
@@ -181,7 +189,7 @@
     def _():
         panel[x, y, core] = rows[slot, 0:32, :]
 
-    pl.semaphore_wait(barrier, 12 + 2 * (STOPS - 1))
+    pl.semaphore_wait(barrier, 14 + 2 * (STOPS - 1))
 
     def copy(view, row, col, send, recv):
         return pltpu.make_async_remote_copy(
@@ -214,13 +222,13 @@
 
     def count(i, total):
         lefts, rights = [], []
-        for r in range(8):
-            left, right = counts_step(jnp.broadcast_to(pairs_ref[pl.ds(i * 8 + r, 1), :], (8, 128))[0:1, :], first)
-            lefts.append(left)
-            rights.append(right)
+        for q in range(4):
+            left, right = counts_step(pairs_ref[pl.ds(pl.multiple_of(i * 32 + q * 8, 8), 8), :], first)
+            lefts += left
+            rights += right
         return total + dot_nt(jnp.concatenate(lefts, axis=1), jnp.concatenate(rights, axis=1))
 
-    hits[:, 0:48] = lax.fori_loop(0, pairs_ref.shape[0] // 8, count, jnp.zeros((48, 48), F32))
+    hits[:, 0:48] = lax.fori_loop(0, pairs_ref.shape[0] // 32, count, jnp.zeros((48, 48), F32))
 
     @pl.when(slot != 0)
     def _():
@@ -257,11 +265,23 @@
         copy(up, me, slot, bs.at[2 * h - 2], br.at[2 * h - 2]).wait_send()
         copy(down, me, slot, bs.at[2 * h - 1], br.at[2 * h - 1]).wait_send()
 
-    def visit(j):
+    def visitor_copy(src, dst, row, i):
         return pltpu.make_async_remote_copy(
-            src_ref=rows.at[slot], dst_ref=rows.at[7 + j], send_sem=vs.at[j - 1], recv_sem=vr.at[j - 1],
-            device_id=((me + j) % 32, slot), device_id_type=MESH,
+            src_ref=rows.at[src], dst_ref=rows.at[dst], send_sem=vs.at[i], recv_sem=vr.at[i],
+            device_id=(row, slot), device_id_type=MESH,
         )
+
+    def visit_next():
+        return visitor_copy(slot, 9, (me + 2) % 32, 0)
+
+    def visit_relay():
+        return visitor_copy(9, 10 - 2 * core, twin, 1)
+
+    def visit_straight():
+        return visitor_copy(slot, 8 + 2 * core, (me + 1 + 2 * core) % 32, 2)
+
+    def visit_arrive(i, at):
+        visitor_copy(at, at, twin, i).wait_recv()
 
     ring_send(1)
     near, far = pl.ds(0, 1024), pl.ds(1024, 1024)
@@ -282,66 +302,87 @@
         c.start()
         passed.append((c, back, i))
 
-    own_near, own_far = panel.at[x, y, core, :, near], panel.at[x, y, core, :, far]
-    send(own_near, to_xp, 0)
-    send(own_far, to_yp, 1)
-    send(own_near, to_xm, 2)
-    send(own_far, to_ym, 3)
+    xs, ys = (x, xp, xo, xm), (y, yp, yo, ym)
+
+    def piece(half, along, across):
+        if half == 0:
+            return panel.at[xs[along], ys[across], core, :, near]
+        return panel.at[xs[across], ys[along], core, :, far]
+
+    first_to = ((to_xp, to_xm), (to_yp, to_ym))
+    far_to = (row_at(xo, y, core), row_at(x, yo, core))
+    second_to = ((to_yp, to_ym), (to_xp, to_xm))
+
+    def second(half, along):
+        for way in range(2):
+            send(piece(half, along, 0), second_to[half][way], 8 + half * 12 + along * 2 + way)
+
+    def second_arrive(half, along, way):
+        arrive(piece(half, along, 3 if way == 0 else 1), 8 + half * 12 + along * 2 + way)
+
+    def second_pass(half, along, way):
+        i = 16 + half * 12 + along
+        send(piece(half, along, 3 if way == 0 else 1), second_to[half][way], i)
+
+    for half in range(2):
+        for way in range(2):
+            send(piece(half, 0, 0), first_to[half][way], half * 4 + way)
+    for half in range(2):
+        send(piece(half, 0, 0), far_to[half], half * 4 + 2)
+    for half in range(2):
+        second(half, 0)
     share(panel.at[x, y, core], panel.at[x, y, 1 - core], 0)
-    top, bottom = pl.ds(0, 16), pl.ds(16, 16)
-    arrive(panel.at[xm, y, core, :, near], 0)
-    send(panel.at[xm, y, core, top, near], to_xp, 4)
-    arrive(panel.at[x, ym, core, :, far], 1)
-    send(panel.at[x, ym, core, top, far], to_yp, 5)
-    arrive(panel.at[xp, y, core, :, near], 2)
-    send(panel.at[xp, y, core, bottom, near], to_xm, 6)
-    arrive(panel.at[x, yp, core, :, far], 3)
-    send(panel.at[x, yp, core, bottom, far], to_ym, 7)
+    for half in range(2):
+        arrive(piece(half, 3, 0), half * 4)
+        arrive(piece(half, 1, 0), half * 4 + 1)
+    for half in range(2):
+        second(half, 3)
+        second(half, 1)
     share(panel.at[xm, y, core, :, near], panel.at[xm, y, 1 - core, :, near], 1)
     share(panel.at[x, ym, core, :, far], panel.at[x, ym, 1 - core, :, far], 2)
     share(panel.at[xp, y, core, :, near], panel.at[xp, y, 1 - core, :, near], 3)
     share(panel.at[x, yp, core, :, far], panel.at[x, yp, 1 - core, :, far], 4)
-    arrive(panel.at[xo, y, core, top, near], 4)
-    arrive(panel.at[xo, y, core, bottom, near], 6)
-    send(panel.at[:, y, core, :, near], to_yp, 8)
-    send(panel.at[:, y, core, :, near], to_ym, 10)
-    arrive(panel.at[x, yo, core, top, far], 5)
-    arrive(panel.at[x, yo, core, bottom, far], 7)
-    send(panel.at[x, :, core, :, far], to_xp, 9)
-    send(panel.at[x, :, core, :, far], to_xm, 11)
+    for half in range(2):
+        second_arrive(half, 0, 0)
+        second_pass(half, 0, 0)
+    for half in range(2):
+        arrive(piece(half, 2, 0), half * 4 + 2)
+        second(half, 2)
     share(panel.at[xo, y, core, :, near], panel.at[xo, y, 1 - core, :, near], 5)
     share(panel.at[x, yo, core, :, far], panel.at[x, yo, 1 - core, :, far], 6)
-
-    ring_arrive(1)
-    ring_send(2)
+    for half in range(2):
+        second_arrive(half, 0, 1)
+        second_arrive(half, 3, 1)
+        second_pass(half, 3, 1)
+        second_arrive(half, 1, 0)
+        second_pass(half, 1, 0)
+
     row_hits = hits[:, 0:48]
     pextra[...] = 0.1 + 0.5 * spread(row_hits[0:32, 0:32], 32)
     extra[...] = 0.1 + 0.5 * spread(row_hits[32:40, 32:48], 16)
 
-    first_two, last_two = pl.ds(0, 2), pl.ds(2, 2)
-    arrive(panel.at[:, ym, core, :, near], 8)
-    send(panel.at[first_two, ym, core, :, near], to_yp, 12)
-    arrive(panel.at[xm, :, core, :, far], 9)
-    send(panel.at[xm, first_two, core, :, far], to_xp, 13)
-    arrive(panel.at[:, yp, core, :, near], 10)
-    send(panel.at[last_two, yp, core, :, near], to_ym, 14)
-    arrive(panel.at[xp, :, core, :, far], 11)
-    send(panel.at[xp, last_two, core, :, far], to_xm, 15)
+    for half in range(2):
+        second_arrive(half, 3, 0)
+        second_arrive(half, 1, 1)
+    for half in range(2):
+        second_arrive(half, 2, 1)
+        second_pass(half, 2, 1)
+        second_arrive(half, 2, 0)
     share(panel.at[:, ym, core, :, near], panel.at[:, ym, 1 - core, :, near], 7)
     share(panel.at[xm, :, core, :, far], panel.at[xm, :, 1 - core, :, far], 8)
     share(panel.at[:, yp, core, :, near], panel.at[:, yp, 1 - core, :, near], 9)
     share(panel.at[xp, :, core, :, far], panel.at[xp, :, 1 - core, :, far], 10)
-    arrive(panel.at[first_two, yo, core, :, near], 12)
-    arrive(panel.at[last_two, yo, core, :, near], 14)
+    ring_arrive(1)
+    ring_send(2)
+    for half in range(2):
+        for along in range(4):
+            arrive(piece(half, along, 2), 16 + half * 12 + along)
     share(panel.at[:, yo, core, :, near], panel.at[:, yo, 1 - core, :, near], 11)
-    arrive(panel.at[xo, first_two, core, :, far], 13)
-    arrive(panel.at[xo, last_two, core, :, far], 15)
     share(panel.at[xo, :, core, :, far], panel.at[xo, :, 1 - core, :, far], 12)
     for c, back, i in passed:
         copy(back, twin, slot, cs.at[i], cr.at[i]).wait_recv()
         c.wait_send()
-    for j in range(1, STOPS):
-        visit(j).start()
+    visit_next().start()
 
     def panel_rows(n):
         return panel[n].reshape(256, 2048)
@@ -370,75 +411,72 @@
     lax.fori_loop(0, SIDE, build, 0)
 
     def event(m):
-        @pl.when(m == RING_THREE)
+        @pl.when(m == 1)
         def _():
             ring_arrive(2)
             ring_send(3)
-
-        @pl.when(m == RING_FOUR)
+            visit_arrive(0, 9)
+            visit_relay().start()
+            visit_straight().start()
+
+        @pl.when(m == 4)
         def _():
             ring_arrive(3)
             ring_send(4)
 
-    chain_steps(a, leaf, low, up, event)
-
-    def finish(k, unused):
-        own = pl.ds(pl.multiple_of(k * LEAF, LEAF), LEAF)
-        row = lax.broadcasted_iota(jnp.int32, (PANEL, LEAF), 0)
-        value = jnp.where(row < (k + 1) * LEAF, a[:, own], 0.0)
-        high, lo = halves(value)
-        xh[:, own] = high
-        xl[:, own] = lo
-        return unused
-
-    lax.fori_loop(0, PANEL // LEAF, finish, 0)
-    ring_arrive(4)
-    for j in range(1, STOPS):
-        visit(j).wait_recv()
-    total = 1024 + 3 * LEAF
-
-    def all_rows():
-        return rows[...].reshape(total, 2048)
-
-    def squares(i, unused):
-        v = rows[i].astype(F32)
-        s = jnp.sum(v * v, axis=1, keepdims=True)
-        sq_col[pl.ds(pl.multiple_of(i * LEAF, LEAF), LEAF), :] = jnp.broadcast_to(s, (LEAF, 128))
-        return unused
-
-    lax.fori_loop(0, total // LEAF, squares, 0)
+        @pl.when(m == 5)
+        def _():
+            visit_arrive(1, 8 + 2 * core)
+            visit_arrive(2, 10 - 2 * core)
+
+        @pl.when(m == 6)
+        def _():
+            ring_arrive(4)
+
+    lead_row = lax.broadcasted_iota(jnp.int32, (32, PANEL), 0)
+    lead_lane = lax.broadcasted_iota(jnp.int32, (32, PANEL), 1)
+
+    def kernel_rows(slices):
+        parts = []
+        for i, block_id, leads in slices:
+            v = rows[i].astype(F32)
+            parts.append(jnp.sum(v * v, axis=1, keepdims=True))
+            sq_col[pl.ds(pl.multiple_of(i * LEAF, LEAF), LEAF), :] = jnp.broadcast_to(parts[-1], (LEAF, 128))
+        left = jnp.concatenate([rows[i] for i, block_id, leads in slices], axis=0)
+        g = dot_nt(left, panel[...].reshape(PANEL, 2048))
+        k = jnp.exp(-0.5 * (jnp.concatenate(parts, axis=0) + psq_row[0:1, :] - 2.0 * g))
+        for q, (i, block_id, leads) in enumerate(slices):
+            hit = lead_lane == block_id * 32 + lead_row
+            top_rows = k[q * LEAF : q * LEAF + 32, :] + jnp.where(hit, pextra[0:1, :] * leads, 0.0)
+            high, lo = halves(jnp.concatenate([top_rows, k[q * LEAF + 32 : (q + 1) * LEAF, :]], axis=0))
+            at = pl.ds(pl.multiple_of(i * LEAF, LEAF), LEAF)
+            kh[at, :] = high
+            kl[at, :] = lo
+
+    def is_zero(i):
+        return jnp.where(i == 0, 1.0, 0.0).astype(F32)
+
+    def one_slice(m):
+        away = (m + 1) // 2
+        i = (slot + 8 + away - 2 * away * (m % 2)) % 8
+        kernel_rows([(i, me, is_zero(i))])
+
+    def two_slices(m):
+        late, last = m // 5, m // 6
+        early = 1 - late
+        i = early * ((slot + 9 - m) % 8) + late * (4 + m)
+        i_block = early * me + late * ((me + 35 - m) % 32)
+        j = early * ((slot + m - 1) % 8) + (late - last) * 8 + last * ((slot + 4) % 8)
+        j_block = (1 - late + last) * me + (late - last) * ((me + 31) % 32)
+        i_slice = early * i + late * slot
+        j_slice = (1 - late + last) * j + (late - last) * slot
+        kernel_rows([(i, i_block, is_zero(i_slice)), (j, j_block, is_zero(j_slice))])
+
+    chain_steps(a, leaf, low, up, xh, xl, event, one_slice, two_slices)
     own = pl.ds(pl.multiple_of(slot * LEAF, LEAF), LEAF)
     sq_row[0:1, 0:128] = sq_col[own, :].T[0:1, :]
     for s in range(3):
         sq_row[0:1, (s + 1) * LEAF : (s + 2) * LEAF] = sq_col[1024 + s * LEAF : 1024 + (s + 1) * LEAF, :].T[0:1, :]
-    lead_row = lax.broadcasted_iota(jnp.int32, (32, 256), 0)
-    lead_lane = lax.broadcasted_iota(jnp.int32, (32, 256), 1)
-
-    def kernel_part(n, unused):
-        cols = pl.ds(pl.multiple_of(n * 256, 256), 256)
-        g = dot_nt(all_rows(), panel_rows(n))
-        s = sq_col[...]
-        k = jnp.exp(-0.5 * (jnp.concatenate([s, s], axis=1) + psq_row[0:1, cols] - 2.0 * g))
-        high, lo = halves(k)
-        kh[:, cols] = high
-        kl[:, cols] = lo
-        more = pextra[0:1, cols]
-
-        def fix(start, block, scale):
-            part = k[start : start + 32, :]
-            hit = lead_lane + n * 256 == block * 32 + lead_row
-            part = part + jnp.where(hit, more * scale, 0.0)
-            high, lo = halves(part)
-            kh[start : start + 32, cols] = high
-            kl[start : start + 32, cols] = lo
-
-        fix(0, me, 1.0)
-        lead = jnp.where(slot == 0, 1.0, 0.0).astype(F32)
-        for s in range(3):
-            fix(1024 + s * LEAF, (me + 31 - s) % 32, lead)
-        return unused
-
-    lax.fori_loop(0, SIDE, kernel_part, 0)
     for n in range(4):
         depth = 256 * (n + 1)
         cols = slice(256 * n, 256 * n + 256)
@@ -474,8 +512,9 @@
     lax.fori_loop(0, 4, tile, 0)
     for h in range(1, 5):
         ring_sent(h)
-    for j in range(1, STOPS):
-        visit(j).wait_send()
+    visit_next().wait_send()
+    visit_relay().wait_send()
+    visit_straight().wait_send()
     for c in sent:
         c.wait_send()
 
@@ -530,8 +569,8 @@
             pltpu.VMEM((STOPS * LEAF, PANEL), BF16),
             pltpu.SemaphoreType.DMA((15,)),
             pltpu.SemaphoreType.DMA((8,)),
-            pltpu.SemaphoreType.DMA((16,)),
-            pltpu.SemaphoreType.DMA((16,)),
+            pltpu.SemaphoreType.DMA((32,)),
+            pltpu.SemaphoreType.DMA((32,)),
             pltpu.SemaphoreType.DMA((13,)),
             pltpu.SemaphoreType.DMA((13,)),
             pltpu.SemaphoreType.DMA((8,)),
@@ -540,7 +579,7 @@
             pltpu.SemaphoreType.DMA((3,)),
         ],
         compiler_params=pltpu.CompilerParams(
-            collective_id=0, has_side_effects=True, vmem_limit_bytes=60 << 20
+            collective_id=0, has_side_effects=True, vmem_limit_bytes=44 << 20
         ),
         name="whole",
     )(embeddings, inverse_scales, pairs)

time: 115 us -> 99.9 us (0.87)
  Pallas kernels: 110 us -> 94.2 us
    pallas_call x1, Pallas kernels: 110 us -> 94.2 us  [whole(): pl.pallas_call(whole_kernel, out_shape=(jax.ShapeDtypeStruct((1024, STOPS...]
    unnamed x4 -> x8, local copies, waits for them, and re-layouts: 3.93 us -> 4.79 us
where the time goes in v5:
time: 99.9 us; the launch traced here: 99.7 us
  Pallas kernels  94.2 us (94%)
  local copies, waits for them, and re-layouts  4.79 us (5%)
    pallas_call x1, Pallas kernels, whole(): pl.pallas_call(whole_kernel, out_shape=(jax.ShapeDtypeStruct((1024, STOPS...  94.2 us
    unnamed x8, local copies, waits for them, and re-layouts  4.79 us

profile of v5, /device:TPU:1, one launch (start us, length us, event | category | flops | bytes accessed | tf_op | source)
XLA Modules:
  0.0 99.7 jit_solution(10540090726582853694)
XLA Ops:
  0.6 0.0 copy-start
  0.6 1.0 %copy-done = bf16[128,2048]{1,0:T(8,128)(2,1)S(1)} copy-done((bf16[128,2048]{1,0:T(8,128)(2,1)S(1)}, bf16[128,2048]{1,0:T(8,128)(2,1)}, u32[]{:S(2)}) %copy-start) | copy-done | bytes 524312
  1.7 0.0 copy-start.1
  1.7 0.9 copy-done.1
  2.6 0.0 copy-start.2
  2.6 0.7 copy-done.2
  3.3 94.2 %whole.1 = (f32[1024,512]{1,0:T(8,128)S(1)}, f32[128,1024]{1,0:T(8,128)S(1)}) custom-call(bf16[128,2048]{1,0:T(8,128)(2,1)S(1)} %copy-done, f32[1,2048]{1,0:T(1,128)S(1)} %bitcast.7, s32[512,128]{1,0:T(8,128)S(1)} %bitcast.6), custom_call_target="tpu_custom_call" | custom-call | tf_op jit(solution)/shard_map/whole/pallas_call | solution.py:540
  97.6 1.3 %copy.8 = f32[1024,512]{1,0:T(8,128)} copy(f32[1024,512]{1,0:T(8,128)S(1)} %get-tuple-element.4) | data formatting | bytes 4194304
  98.9 0.8 copy.9
Async XLA Ops:
  0.6 1.0 %copy-start = (bf16[128,2048]{1,0:T(8,128)(2,1)S(1)}, bf16[128,2048]{1,0:T(8,128)(2,1)}, u32[]{:S(2)}) copy-start(bf16[128,2048]{1,0:T(8,128)(2,1)} %emb_ref.1) | copy-start | bytes 1572868
  1.7 0.9 copy-start.1
  2.6 0.7 copy-start.2

commit v6 on v5

--- a/solution.py
+++ b/solution.py
@@ -391,15 +391,16 @@
         for q in range(2):
             v = panel_rows(n)[q * LEAF : (q + 1) * LEAF, :].astype(F32)
             s = jnp.sum(v * v, axis=1, keepdims=True)
-            at = pl.ds(pl.multiple_of(n * 256 + q * LEAF, LEAF), LEAF)
+            at = slice(n * 256 + q * LEAF, n * 256 + (q + 1) * LEAF)
             psq_col[at, :] = jnp.broadcast_to(s, (LEAF, 128))
             psq_row[0:1, at] = to_lanes(s)
         return unused
 
-    lax.fori_loop(0, SIDE, panel_squares, 0)
+    for n in range(SIDE):
+        panel_squares(n, 0)
 
     def build(n, unused):
-        cols = pl.ds(pl.multiple_of(n * 256, 256), 256)
+        cols = slice(n * 256, n * 256 + 256)
         g = dot_nt(panel[...].reshape(PANEL, 2048), panel_rows(n))
         s = psq_col[...]
         k = jnp.exp(-0.5 * (jnp.concatenate([s, s], axis=1) + psq_row[0:1, cols] - 2.0 * g))
@@ -408,7 +409,8 @@
         a[:, cols] = k + jnp.where(row == lane + n * 256, pextra[0:1, cols], 0.0)
         return unused
 
-    lax.fori_loop(0, SIDE, build, 0)
+    for n in range(SIDE):
+        build(n, 0)
 
     def event(m):
         @pl.when(m == 1)
@@ -491,25 +493,24 @@
     vl[0:LEAF, :] = fl[own, :]
     vh[LEAF:, :] = fh[1024:, :]
     vl[LEAF:, :] = fl[1024:, :]
-    r = lax.broadcasted_iota(jnp.int32, (256, LEAF), 0)
-    c = lax.broadcasted_iota(jnp.int32, (256, LEAF), 1)
-
-    def tile(i, unused):
-        at = pl.ds(pl.multiple_of(i * 256, 256), 256)
-        left = rows[pl.ds(2 * i, 2)].reshape(256, 2048)
-        g = jnp.concatenate([dot_nt(left, rows[slot]), dot_nt(left, rows[8:11].reshape(3 * LEAF, 2048))], axis=1)
-        s = sq_col[at, :]
-        k = jnp.exp(-0.5 * (jnp.concatenate([s] * 4, axis=1) + sq_row[...] - 2.0 * g))
-        ff = dot_nt(fh[at, :], vh[...])
-        ff = ff + dot_nt(fh[at, :], vl[...])
-        ff = ff + dot_nt(fl[at, :], vh[...])
+    r = lax.broadcasted_iota(jnp.int32, (1024, LEAF), 0)
+    c = lax.broadcasted_iota(jnp.int32, (1024, LEAF), 1)
+
+    def tile(h, unused):
+        at = pl.ds(pl.multiple_of(h * 256, 256), 256)
+        right = jnp.concatenate([rows[(1 - h) * slot + 9 * h], rows[8 + 2 * h]], axis=0)
+        g = dot_nt(rows[0:8].reshape(1024, 2048), right)
+        s = sq_col[0:1024, :]
+        k = jnp.exp(-0.5 * (jnp.concatenate([s, s], axis=1) + sq_row[0:1, at] - 2.0 * g))
+        ff = dot_nt(fh[0:1024, :], vh[at, :])
+        ff = ff + dot_nt(fh[0:1024, :], vl[at, :])
+        ff = ff + dot_nt(fl[0:1024, :], vh[at, :])
         t = k - ff
-        trail_ref[at, :] = t
-        diagonal = jnp.where(r + i * 256 == c + slot * LEAF, extra[0:1, :], 0.0)
-        trail_ref[at, 0:LEAF] = t[:, 0:LEAF] + diagonal
+        diagonal = jnp.where(r == c + slot * LEAF, extra[0:1, :] * jnp.where(h == 0, 1.0, 0.0).astype(F32), 0.0)
+        trail_ref[:, at] = jnp.concatenate([t[:, 0:LEAF] + diagonal, t[:, LEAF:]], axis=1)
         return unused
 
-    lax.fori_loop(0, 4, tile, 0)
+    lax.fori_loop(0, 2, tile, 0)
     for h in range(1, 5):
         ring_sent(h)
     visit_next().wait_send()

time: 99.9 us -> 97.4 us (0.975)
  Pallas kernels: 94.2 us -> 91.6 us
    pallas_call x1, Pallas kernels: 94.2 us -> 91.6 us  [whole(): pl.pallas_call(whole_kernel, out_shape=(jax.ShapeDtypeStruct((1024, STOPS...]
where the time goes in v6:
time: 97.4 us; the launch traced here: 97.1 us
  Pallas kernels  91.6 us (94%)
  local copies, waits for them, and re-layouts  4.79 us (5%)
    pallas_call x1, Pallas kernels, whole(): pl.pallas_call(whole_kernel, out_shape=(jax.ShapeDtypeStruct((1024, STOPS...  91.6 us
    unnamed x8, local copies, waits for them, and re-layouts  4.79 us

profile of v6, /device:TPU:1, one launch (start us, length us, event | category | flops | bytes accessed | tf_op | source)
XLA Modules:
  0.0 97.1 jit_solution(15984856954159852898)
XLA Ops:
  0.6 0.0 copy-start
  0.6 1.0 %copy-done = bf16[128,2048]{1,0:T(8,128)(2,1)S(1)} copy-done((bf16[128,2048]{1,0:T(8,128)(2,1)S(1)}, bf16[128,2048]{1,0:T(8,128)(2,1)}, u32[]{:S(2)}) %copy-start) | copy-done | bytes 524312
  1.7 0.0 copy-start.1
  1.7 0.9 copy-done.1
  2.6 0.0 copy-start.2
  2.6 0.7 copy-done.2
  3.3 91.6 %whole.1 = (f32[1024,512]{1,0:T(8,128)S(1)}, f32[128,1024]{1,0:T(8,128)S(1)}) custom-call(bf16[128,2048]{1,0:T(8,128)(2,1)S(1)} %copy-done, f32[1,2048]{1,0:T(1,128)S(1)} %bitcast.7, s32[512,128]{1,0:T(8,128)S(1)} %bitcast.6), custom_call_target="tpu_custom_call" | custom-call | tf_op jit(solution)/shard_map/whole/pallas_call | solution.py:541
  95.0 1.3 %copy.8 = f32[1024,512]{1,0:T(8,128)} copy(f32[1024,512]{1,0:T(8,128)S(1)} %get-tuple-element.4) | data formatting | bytes 4194304
  96.3 0.8 copy.9
Async XLA Ops:
  0.6 1.0 %copy-start = (bf16[128,2048]{1,0:T(8,128)(2,1)S(1)}, bf16[128,2048]{1,0:T(8,128)(2,1)}, u32[]{:S(2)}) copy-start(bf16[128,2048]{1,0:T(8,128)(2,1)} %emb_ref.1) | copy-start | bytes 1572868
  1.7 0.9 copy-start.1
  2.6 0.7 copy-start.2

commit v7 on v6

--- a/solution.py
+++ b/solution.py
@@ -304,10 +304,10 @@
 
     xs, ys = (x, xp, xo, xm), (y, yp, yo, ym)
 
-    def piece(half, along, across):
+    def piece(half, along, across, which=core):
         if half == 0:
-            return panel.at[xs[along], ys[across], core, :, near]
-        return panel.at[xs[across], ys[along], core, :, far]
+            return panel.at[xs[along], ys[across], which, :, near]
+        return panel.at[xs[across], ys[along], which, :, far]
 
     first_to = ((to_xp, to_xm), (to_yp, to_ym))
     far_to = (row_at(xo, y, core), row_at(x, yo, core))
@@ -374,11 +374,10 @@
     share(panel.at[xp, :, core, :, far], panel.at[xp, :, 1 - core, :, far], 10)
     ring_arrive(1)
     ring_send(2)
-    for half in range(2):
-        for along in range(4):
+    for along in (0, 3, 1, 2):
+        for half in range(2):
             arrive(piece(half, along, 2), 16 + half * 12 + along)
-    share(panel.at[:, yo, core, :, near], panel.at[:, yo, 1 - core, :, near], 11)
-    share(panel.at[xo, :, core, :, far], panel.at[xo, :, 1 - core, :, far], 12)
+            share(piece(half, along, 2), piece(half, along, 2, 1 - core), 11 + half * 4 + along)
     for c, back, i in passed:
         copy(back, twin, slot, cs.at[i], cr.at[i]).wait_recv()
         c.wait_send()
@@ -572,8 +571,8 @@
             pltpu.SemaphoreType.DMA((8,)),
             pltpu.SemaphoreType.DMA((32,)),
             pltpu.SemaphoreType.DMA((32,)),
-            pltpu.SemaphoreType.DMA((13,)),
-            pltpu.SemaphoreType.DMA((13,)),
+            pltpu.SemaphoreType.DMA((19,)),
+            pltpu.SemaphoreType.DMA((19,)),
             pltpu.SemaphoreType.DMA((8,)),
             pltpu.SemaphoreType.DMA((8,)),
             pltpu.SemaphoreType.DMA((3,)),

time: 97.4 us -> 97.4 us (level)
  no operation moved by 1% of the time
where the time goes in v7:
time: 97.4 us; the launch traced here: 97.2 us
  Pallas kernels  91.7 us (94%)
  local copies, waits for them, and re-layouts  4.79 us (5%)
    pallas_call x1, Pallas kernels, whole(): pl.pallas_call(whole_kernel, out_shape=(jax.ShapeDtypeStruct((1024, STOPS...  91.7 us
    unnamed x8, local copies, waits for them, and re-layouts  4.79 us

profile of v7, /device:TPU:1, one launch (start us, length us, event | category | flops | bytes accessed | tf_op | source)
XLA Modules:
  0.0 97.2 jit_solution(14038625720587766305)
XLA Ops:
  0.6 0.0 copy-start
  0.6 1.0 %copy-done = bf16[128,2048]{1,0:T(8,128)(2,1)S(1)} copy-done((bf16[128,2048]{1,0:T(8,128)(2,1)S(1)}, bf16[128,2048]{1,0:T(8,128)(2,1)}, u32[]{:S(2)}) %copy-start) | copy-done | bytes 524312
  1.7 0.0 copy-start.1
  1.7 0.9 copy-done.1
  2.6 0.0 copy-start.2
  2.6 0.7 copy-done.2
  3.3 91.7 %whole.1 = (f32[1024,512]{1,0:T(8,128)S(1)}, f32[128,1024]{1,0:T(8,128)S(1)}) custom-call(bf16[128,2048]{1,0:T(8,128)(2,1)S(1)} %copy-done, f32[1,2048]{1,0:T(1,128)S(1)} %bitcast.7, s32[512,128]{1,0:T(8,128)S(1)} %bitcast.6), custom_call_target="tpu_custom_call" | custom-call | tf_op jit(solution)/shard_map/whole/pallas_call | solution.py:540
  95.0 1.3 %copy.8 = f32[1024,512]{1,0:T(8,128)} copy(f32[1024,512]{1,0:T(8,128)S(1)} %get-tuple-element.4) | data formatting | bytes 4194304
  96.4 0.8 copy.9
Async XLA Ops:
  0.6 1.0 %copy-start = (bf16[128,2048]{1,0:T(8,128)(2,1)S(1)}, bf16[128,2048]{1,0:T(8,128)(2,1)}, u32[]{:S(2)}) copy-start(bf16[128,2048]{1,0:T(8,128)(2,1)} %emb_ref.1) | copy-start | bytes 1572868
  1.7 0.9 copy-start.1
  2.6 0.7 copy-start.2
